TPU v7x, 32 devices: a whole 2x2x4 slice. The times are simulated.
32 devices in a mesh: groups: 2 (over y), dp: 4 (over x, core), tensor: 4 (over z).
Axes of the slice: x: 2, y: 2, z: 4, core: 2. Of those that a mesh axis runs over, the one named last changes fastest.
Arguments:
- row_adapter_index: int32 [192], P(('groups', 'dp')), parts along dimension 0, may hold values from 0 to 63
- adapter_storage_row: int32 [64], replicated, may hold values from 0 to 63, each once
- initial_head_state: bfloat16 [192, 128, 64, 128], P(('groups', 'dp'), 'tensor'), parts along dimension 0, may hold values from -0.59765625 to 0.59765625
- step_head_input: bfloat16 [4, 192, 8192], P(None, ('groups', 'dp'), 'tensor'), parts along dimension 1, may hold values from -20 to 20
- step_gate_input: bfloat16 [4, 192, 8192], P(None, ('groups', 'dp'), 'tensor'), parts along dimension 1, may hold values from -6 to 6
- step_size_logits: float32 [4, 192, 128], P(None, ('groups', 'dp'), 'tensor'), parts along dimension 1, may hold values from -6 to 6
- state_write_key: bfloat16 [4, 192, 128], P(None, ('groups', 'dp')), parts along dimension 1, may hold values from -0.5 to 0.5
- state_read_query: bfloat16 [4, 192, 128], P(None, ('groups', 'dp')), parts along dimension 1, may hold values from -6 to 6
- head_decay_rate: float32 [128], P('tensor'), may hold values from 0.03 to 3
- head_skip_gain: float32 [128], P('tensor'), may hold values from 0.5 to 1.5
- gated_norm_gain: float32 [8192], P('tensor'), may hold values from 0.1 to 1.9
- output_weight: bfloat16 [8192, 4096], P('tensor'), may hold values from -0.0625 to 0.0625
- adapter_down_weight: bfloat16 [64, 8192, 64], P('dp', 'tensor'), may hold values from -0.0625 to 0.0625
- adapter_up_weight: bfloat16 [64, 64, 4096], P('dp', None, 'tensor'), may hold values from -0.75 to 0.75
Outputs:
- mixed_out: bfloat16 [4, 192, 4096], P(None, ('groups', 'dp'), 'tensor'), parts along dimension 1
- new_state: bfloat16 [192, 128, 64, 128], P(('groups', 'dp'), 'tensor'), parts along dimension 0
There are 2 independent parts, one for each index of `groups`. A program takes and returns all parts, laid end to end along the dimension named above; an argument that names none is the same for every part. Nothing has to cross between parts.
Inputs may be any that keep to these rules, and one draw needn't show every extreme that they name: Row r uses the adapter row_adapter_index[r]. A permutation: adapter a is stored in row adapter_storage_row[a] of adapter_down_weight and adapter_up_weight.
All inputs are finite; a program needn't handle non-finite values.
Results may differ from a plain program's by a relative error of at most 0.009.
Values may be sent and summed in bfloat16 or wider, within the bound.
No kernel may reach another device: no remote copies, remote signals or barrier semaphores. Data moves between devices by JAX's collectives and lax.ppermute only.
A program may use at most 128 MiB of HBM per device.

v0:
```python
import jax
import jax.numpy as jnp
from jax import lax
from jax.sharding import PartitionSpec as P

STATE_HEADS = 128
HEAD_WIDTH = 64


EPSILON = 1e-05


def slot_lookup(row_adapter_index, adapter_storage_row):
    match = row_adapter_index[:, None] == lax.broadcasted_iota(
        jnp.int32, (row_adapter_index.shape[0], adapter_storage_row.shape[0]), 1
    )
    return jnp.sum(jnp.where(match, adapter_storage_row[None, :], 0), axis=1)


def per_device(
    row_adapter_index,
    adapter_storage_row,
    initial_head_state,
    step_head_input,
    step_gate_input,
    step_size_logits,
    state_write_key,
    state_read_query,
    head_decay_rate,
    head_skip_gain,
    gated_norm_gain,
    output_weight,
    adapter_down_weight,
    adapter_up_weight,
):
    steps_n, row_count, width = step_head_input.shape
    head_count = head_decay_rate.shape[0]
    head_dim = width // head_count
    carried = initial_head_state
    gated_list = []
    for moment in range(steps_n):
        delta_t = jax.nn.softplus(step_size_logits[moment])
        damping = jnp.exp(-delta_t * head_decay_rate[None, :])
        values = (
            step_head_input[moment].astype(jnp.float32).reshape(row_count, head_count, head_dim)
        )
        writer = state_write_key[moment].astype(jnp.float32)
        reader = state_read_query[moment].astype(jnp.float32)
        updated = (
            damping[:, :, None, None] * carried.astype(jnp.float32)
            + (delta_t[:, :, None] * values)[:, :, :, None] * writer[:, None, None, :]
        )
        carried = updated.astype(jnp.bfloat16)
        output = (
            jnp.sum(updated * reader[:, None, None, :], axis=3)
            + head_skip_gain[None, :, None] * values
        )
        gated_list.append(
            output.reshape(row_count, width)
            * jax.nn.silu(step_gate_input[moment].astype(jnp.float32))
        )
    gated_all = jnp.stack(gated_list)
    totals = lax.psum(jnp.sum(gated_all * gated_all, axis=2), "tensor")
    scaling = lax.rsqrt(totals / (STATE_HEADS * HEAD_WIDTH) + EPSILON)
    normed = (gated_all * scaling[:, :, None] * gated_norm_gain[None, None, :]).astype(jnp.bfloat16)
    base = jnp.dot(
        normed.reshape(steps_n * row_count, width),
        output_weight,
        preferred_element_type=jnp.float32,
    )
    base = lax.psum_scatter(
        base.reshape(steps_n, row_count, -1), "tensor", scatter_dimension=2, tiled=True
    )
    running_state = adapter_down_weight.shape[0]
    slots = slot_lookup(row_adapter_index, adapter_storage_row)
    columns = lax.broadcasted_iota(jnp.int32, (row_count, adapter_storage_row.shape[0]), 1)
    marks = (slots[:, None] == columns).astype(jnp.bfloat16)
    normed_steps_list, every_mark = (
        lax.all_gather(normed, "dp", axis=1, tiled=True),
        lax.all_gather(marks, "dp", axis=0, tiled=True),
    )
    owned = lax.dynamic_slice_in_dim(
        every_mark, lax.axis_index("dp") * running_state, running_state, 1
    )
    partial_down = jnp.einsum(
        "pcu,oue->pcoe", normed_steps_list, adapter_down_weight, preferred_element_type=jnp.float32
    )
    picked = jnp.sum(partial_down * owned.astype(jnp.float32)[None, :, :, None], axis=2)
    down_projected = lax.psum(picked, "tensor").astype(jnp.bfloat16)
    up_projected = down_projected[:, :, None, :] * owned[None, :, :, None]
    adapter_delta = jnp.einsum(
        "bcuo,uoz->bcz", up_projected, adapter_up_weight, preferred_element_type=jnp.float32
    )
    adapter_delta = lax.psum_scatter(adapter_delta, "dp", scatter_dimension=1, tiled=True)
    mixed_out = (base + adapter_delta).astype(jnp.bfloat16)
    return (mixed_out, carried)


def solution(mesh):
    placed = (
        P(("groups", "dp")),
        P(),
        P(("groups", "dp"), "tensor", None, None),
        P(None, ("groups", "dp"), "tensor"),
        P(None, ("groups", "dp"), "tensor"),
        P(None, ("groups", "dp"), "tensor"),
        P(None, ("groups", "dp"), None),
        P(None, ("groups", "dp"), None),
        P("tensor"),
        P("tensor"),
        P("tensor"),
        P("tensor", None),
        P("dp", "tensor", None),
        P("dp", None, "tensor"),
    )
    return jax.shard_map(
        per_device,
        mesh=mesh,
        in_specs=placed,
        out_specs=(P(None, ("groups", "dp"), "tensor"), P(("groups", "dp"), "tensor", None, None)),
        check_vma=False,
    )
```

profile of v0, /device:TPU:0, one launch (start us, length us, event | category | flops | bytes accessed | tf_op | source)
XLA Modules:
  0.0 183.1 jit_solution(18345866340556705765)
XLA Ops:
  8.1 1.2 slice_convert_fusion
  9.3 0.2 reshape.387
  9.5 0.9 reshape.390
  10.4 0.2 reshape.393
  10.6 0.2 reshape.396
  10.7 0.8 multiply_exponential_fusion
  11.6 0.8 bitcast_convert_fusion.1
  12.4 2.2 %broadcast_multiply_fusion.2 = (f32[24,32,64]{2,1,0:T(8,128)}, f32[24,32,64]{2,1,0:T(8,128)}) fusion(f32[24,32,64]{2,1,0:T(8,128)} %reshape.390, f32[24,32]{1,0:T(8,128)S(1)} %get-tuple-element.19, f32[24,32,64]{2,1,0:T(8,128)S(1)} %reshape.387, f32[24,32]{1,0:T(8,128)S(1)} %get-tuple-element.20), kind=kLoop, calls=%fused_computation.54 | loop fusion | flops 98304 | bytes 792576 | tf_op jit(solution)/shard_map/mul | solution.py:51
  14.6 1.1 broadcast_multiply_fusion
  15.7 62.2 %multiply_reduce_fusion.1 = (f32[24,32,64]{2,1,0:T(8,128)S(1)}, f32[24,32,64]{2,1,0:T(8,128)S(1)}, f32[24,32,64]{2,1,0:T(8,128)S(1)}, f32[24,32,64]{2,1,0:T(8,128)}, bf16[24,32,64,128]{3,2,1,0:T(8,128)(2,1)}) fusion(f32[24,128]{1,0:T(8,128)S(1)} %get-tuple-element.35, f32[24,128]{1,0:T(8,128)S(1)} %get-tuple-element.30, f32[24,32,64]{2,1,0:T(8,128)} %get-tuple-element.32, ...), kind=kLoop, calls=%fused_computation.3 | loop fusion | flops 175964160 | bytes 26849280 | tf_op jit(solution)/shard_map/reduce_sum | solution.py:55
  77.9 1.2 reduce_sum.72
  79.1 0.8 reduce_sum.74
  80.3 1.5 fusion.22
  82.0 13.5 %psum.14 = f32[4,24]{1,0:T(4,128)S(1)} all-reduce(f32[4,24]{1,0:T(4,128)S(1)} %multiply_reduce_fusion.5), channel_id=1, replica_groups=mesh['groups'=2,'dp'=4,'tensor'=4] {'tensor'}, use_global_device_ids=true, to_apply=%region_5.6 | all-reduce | flops 96 | bytes 768 | tf_op jit(solution)/shard_map/psum | solution.py:63
  95.5 0.9 multiply_convert_fusion
  96.4 10.2 %fusion.4 = f32[4,24,4096]{2,1,0:T(8,128)} fusion(bf16[4,24,2048]{2,1,0:T(8,128)(2,1)} %multiply_convert_fusion, bf16[2048,4096]{1,0:T(8,128)(2,1)} %param.25), kind=kOutput, calls=%fused_computation.12 | convolution fusion | flops 1610612736 | bytes 18743296 | tf_op jit(solution)/shard_map/dot_general | solution.py:66
  106.7 0.2 select_reduce_fusion
  107.0 5.3 %all_gather.7 = bf16[96,64]{1,0:T(8,128)(2,1)S(1)} all-gather(bf16[24,64]{1,0:T(8,128)(2,1)S(1)} %fusion.51), channel_id=1, replica_groups=mesh['groups'=2,'dp'=4,'tensor'=4] {'dp'}, dimensions={0}, use_global_device_ids=true | all-gather | bytes 15360 | tf_op jit(solution)/shard_map/all_gather | solution.py:80
  112.4 2.1 %all-gather.2.cloned.1.call-done = bf16[4,96,2048]{2,1,0:T(8,128)(2,1)} async-done(((bf16[4,24,2048]{2,1,0:T(8,128)(2,1)}), bf16[4,96,2048]{2,1,0:T(8,128)(2,1)}) %all-gather.2.cloned.1.call-update) | async-done | bytes 1572880 | tf_op jit(solution)/shard_map/all_gather | solution.py:79
  114.5 5.0 %multiply_reduce_fusion.4 = f32[4,96,64]{1,2,0:T(8,128)S(1)} fusion(bf16[16,2048,64]{1,2,0:T(8,128)(2,1)} %param.26, bf16[4,96,2048]{2,1,0:T(8,128)(2,1)} %all-gather.2.cloned.1.call-done, f32[96,16]{0,1:T(8,128)S(1)} %convert_element_type.238), kind=kOutput, calls=%fused_computation.18 | convolution fusion | flops 1611374592 | bytes 5871616 | tf_op jit(solution)/shard_map/pcu,oue->pcoe/dot_general | solution.py:85
  119.6 25.3 %psum.15 = bf16[4,96,64]{1,2,0:T(8,128)(2,1)S(1)} all-reduce(f32[4,96,64]{1,2,0:T(8,128)S(1)} %multiply_reduce_fusion.4), channel_id=1, replica_groups=mesh['groups'=2,'dp'=4,'tensor'=4] {'tensor'}, use_global_device_ids=true, to_apply=%region_9.10 | all-reduce | flops 24576 | bytes 147456 | tf_op jit(solution)/shard_map/psum | solution.py:89
  144.9 2.2 %fusion.13 = f32[4,96,1024]{2,1,0:T(8,128)} fusion(bf16[16,64,1024]{2,1,0:T(8,128)(2,1)S(1)} %copy-done, bf16[96,16]{0,1:T(8,128)(2,1)S(1)} %copy.23, bf16[4,96,64]{1,2,0:T(8,128)(2,1)S(1)} %psum.15), kind=kOutput, calls=%fused_computation.20 | convolution fusion | flops 805699584 | bytes 3722240 | tf_op jit(solution)/shard_map/bcuo,uoz->bcz/dot_general | solution.py:91
  147.1 26.7 %reduce-scatter.5.cloned.1.call-done = f32[4,24,1024]{2,1,0:T(8,128)} async-done(((f32[4,96,1024]{2,1,0:T(8,128)}), f32[4,24,1024]{2,1,0:T(8,128)}) %reduce-scatter.5.cloned.1.call-update) | async-done | bytes 393232 | tf_op jit(solution)/shard_map/reduce_scatter | solution.py:94
  173.8 1.8 %add_convert_fusion = bf16[4,24,1024]{2,1,0:T(8,128)(2,1)} fusion(f32[4,24,1024]{2,1,0:T(8,128)} %reduce-scatter.3.cloned.1.call-done, f32[4,24,1024]{2,1,0:T(8,128)} %reduce-scatter.5.cloned.1.call-done), kind=kLoop, calls=%fused_computation.27 | loop fusion | flops 196608 | bytes 983040 | tf_op jit(solution)/shard_map/convert_element_type | solution.py:95
  (27 shorter events, 1.0 us)
Async XLA Ops:
  8.0 136.9 %copy-start = (bf16[16,64,1024]{2,1,0:T(8,128)(2,1)S(1)}, bf16[16,64,1024]{2,1,0:T(8,128)(2,1)}, u32[]{:S(2)}) copy-start(bf16[16,64,1024]{2,1,0:T(8,128)(2,1)} %param.27) | copy-start | bytes 6291460
  8.0 106.5 %all-gather.2.cloned.1.call-start = ((), (), s32[]{:S(2)}) async-start(), calls=%async_computation.3 | async-start | bytes 1966080 | tf_op jit(solution)/shard_map/all_gather | solution.py:79
  12.4 67.8 %copy-start.2 = (f32[32]{0:T(128)S(1)}, f32[32]{0:T(128)}, u32[]{:S(2)}) copy-start(f32[32]{0:T(128)} %param.23) | copy-start | bytes 388
  15.7 79.8 %copy-start.1 = (f32[2048]{0:T(1024)S(1)}, f32[2048]{0:T(1024)}, u32[]{:S(2)}) copy-start(f32[2048]{0:T(1024)} %param.24) | copy-start | bytes 24580
  77.9 28.8 %copy-start.3 = (s32[64]{0:T(128)S(1)}, s32[64]{0:T(128)}, u32[]{:S(2)}) copy-start(s32[64]{0:T(128)} %param.15) | copy-start | bytes 772
  77.9 28.8 %copy-start.4 = (s32[24]{0:T(128)S(1)}, s32[24]{0:T(128)}, u32[]{:S(2)}) copy-start(s32[24]{0:T(128)} %param.14) | copy-start | bytes 292
  96.4 50.7 %reduce-scatter.3.cloned.1.call-start = ((), (), s32[]{:S(2)}) async-start(), calls=%async_computation.2 | async-start | bytes 1966080 | tf_op jit(solution)/shard_map/reduce_scatter | solution.py:71
  106.6 67.2 %reduce-scatter.5.cloned.1.call-start = ((), (), s32[]{:S(2)}) async-start(), calls=%async_computation.4 | async-start | bytes 1966080 | tf_op jit(solution)/shard_map/reduce_scatter | solution.py:94
Sparse Core Ops, SparseCore 0:
  96.5 17.9 all-gather.1
Sparse Core Ops, SparseCore 1:
  106.7 37.2 reduce-scatter.2
  147.2 26.5 reduce-scatter.4
where the time goes:
time: 183 us
  other arithmetic  73.1 us (40%)
  blocking collectives  44.1 us (24%)
  waiting for transfers between devices  28.9 us (16%)
  matrix products  17.4 us (10%)
  between operations  15.6 us (9%)
  local copies, waits for them, and re-layouts  3.98 us (2%)
    reduce_sum x1, other arithmetic, per_device(): jnp.sum(updated * reader[:, None, None, :], axis=3)  62.2 us
    reduce_scatter x1, waiting for transfers between devices, per_device(): lax.psum_scatter(adapter_delta, 'dp', scatter_dimension=1, tiled=True)  26.7 us
    psum x1, blocking collectives, per_device(): down_projected = lax.psum(picked, 'tensor').astype(jnp.bfloat16)  25.3 us
    psum x1, blocking collectives, per_device(): totals = lax.psum(jnp.sum(gated_all * gated_all, axis=2), 'tensor')  13.5 us
    dot_general x1, matrix products, per_device(): jnp.dot(normed.reshape(steps_n * row_count, width), output_weight, prefer...  10.2 us
    all_gather x1, blocking collectives, per_device(): lax.all_gather(marks, 'dp', axis=0, tiled=True)  5.28 us
    dot_general x1, matrix products, per_device(): jnp.einsum('pcu,oue->pcoe', normed_steps_list, adapter_down_weight, prefe...  5.03 us
  transfers between devices with their start and end apart: 3, of which 2 were waited for; matrix products, arithmetic and copies ran while one was open for 10% of the time, Pallas kernels for 0%

commit v1 on v0

--- a/solution.py
+++ b/solution.py
@@ -1,13 +1,476 @@
+import functools
+
 import jax
 import jax.numpy as jnp
 from jax import lax
+from jax.experimental import pallas as pl
+from jax.experimental.pallas import tpu as pltpu
 from jax.sharding import PartitionSpec as P
 
 STATE_HEADS = 128
 HEAD_WIDTH = 64
-
-
 EPSILON = 1e-05
+
+BF = jnp.bfloat16
+F32 = jnp.float32
+NT = (((1,), (1,)), ((), ()))
+TN = (((0,), (0,)), ((), ()))
+NN = (((1,), (0,)), ((), ()))
+LANES = 128
+EXT = 16
+
+
+def dot(a, b, dims=NN):
+    return lax.dot_general(a, b, dims, preferred_element_type=F32)
+
+
+def state_body(
+    first_block, with_slots, hb, steps, rows, heads, *refs
+):
+    refs = list(refs)
+    if with_slots:
+        idx_ref, store_ref = refs.pop(0), refs.pop(0)
+    (x_ref, g_ref, lg_ref, rate_ref, skip_ref, gain_ref, w_ref, q_ref, s_ref) = refs[:9]
+    refs = refs[9:]
+    if not with_slots:
+        refs = refs[1:]
+    ns_ref, u_ref, ss_ref = refs[:3]
+    chi_ref, clo_ref, wbd_ref, qbd_ref, k4_ref, slot_ref = refs[3:]
+    j = pl.program_id(0)
+    tr = steps * rows
+    cols = hb * HEAD_WIDTH
+    n = w_ref.shape[2]
+    pairs = rows // 2
+
+    @pl.when(j == 0)
+    def _():
+        delta = [jax.nn.softplus(lg_ref[t]) for t in range(steps)]
+        keep = [jnp.exp(-delta[t] * rate_ref[...]) for t in range(steps)]
+        w = [w_ref[t].astype(F32) for t in range(steps)]
+        q = [q_ref[t].astype(F32) for t in range(steps)]
+        cum = []
+        for t in range(steps):
+            cum.append(keep[t] if t == 0 else cum[-1] * keep[t])
+        c = [delta[s] for s in range(steps)]
+        coef = list(cum)
+        cur = []
+        for t in range(steps):
+            cur = [v * keep[t] for v in cur] + [delta[t]]
+            for s in range(t + 1):
+                dotted = jnp.sum(w[s] * q[t], axis=1, keepdims=True)
+                a = cur[s] * dotted
+                if s == t:
+                    a = a + skip_ref[...]
+                coef.append(a)
+        coef += cur
+        coef = jnp.concatenate(coef, axis=0)
+        hi = coef.astype(BF)
+        chi_ref[...] = hi
+        clo_ref[...] = (coef - hi.astype(F32)).astype(BF)
+        eye = lax.broadcasted_iota(jnp.int32, (heads, heads), 0) == lax.broadcasted_iota(
+            jnp.int32, (heads, heads), 1
+        )
+        for r in range(rows):
+            col = jnp.sum(jnp.where(eye, cum[-1][r : r + 1, :], 0.0), axis=1, keepdims=True)
+            k4_ref[r] = jnp.broadcast_to(col, (heads, LANES))
+        wf = jnp.concatenate(w, axis=0)
+        qf = jnp.concatenate(q, axis=0)
+        owner = lax.rem(lax.broadcasted_iota(jnp.int32, (tr, n), 0), rows)
+        for p in range(pairs):
+            for half in range(2):
+                mine = owner == 2 * p + half
+                wbd_ref[p, :, half * n : (half + 1) * n] = jnp.where(mine, wf, 0.0).astype(BF)
+                qbd_ref[p, :, half * n : (half + 1) * n] = jnp.where(mine, qf, 0.0).astype(BF)
+        ss_ref[...] = jnp.zeros_like(ss_ref)
+        if with_slots:
+            for r in range(rows):
+                slot = store_ref[idx_ref[r]].astype(F32)
+                for t in range(steps):
+                    slot_ref[t * rows + r : t * rows + r + 1, :] = jnp.full((1, LANES), slot, F32)
+            for b in range(u_ref.shape[1] // LANES):
+                lo = min(b * EXT, tr - EXT)
+                u_ref[tr : tr + EXT, b * LANES : (b + 1) * LANES] = slot_ref[lo : lo + EXT, :].astype(BF)
+
+    block = first_block + j
+    hsel = lax.broadcasted_iota(jnp.int32, (heads, cols), 0)
+    hcol = lax.broadcasted_iota(jnp.int32, (heads, cols), 1) // HEAD_WIDTH + block * hb
+    expand = jnp.where(hsel == hcol, 1.0, 0.0).astype(BF)
+    ce = dot(chi_ref[...], expand) + dot(clo_ref[...], expand)
+    x = [x_ref[t].astype(F32) for t in range(steps)]
+    last = ce.shape[0] - tr
+    xe = jnp.concatenate(
+        [ce[last + s * rows : last + (s + 1) * rows] * x[s] for s in range(steps)], axis=0
+    )
+    xet = xe.T.astype(BF)
+    z = jnp.zeros((tr, cols), F32)
+    for p in range(pairs):
+        s0 = s_ref[2 * p].reshape(cols, n)
+        s1 = s_ref[2 * p + 1].reshape(cols, n)
+        z = z + dot(qbd_ref[p], jnp.concatenate([s0, s1], axis=1), NT)
+        up = dot(xet, wbd_ref[p])
+        for half, sv in ((0, s0), (1, s1)):
+            r = 2 * p + half
+            k4 = k4_ref[r, pl.ds(block * hb, hb), :]
+            grown = (
+                k4[:, None, :] * sv.astype(F32).reshape(hb, HEAD_WIDTH, n)
+                + up[:, half * n : (half + 1) * n].reshape(hb, HEAD_WIDTH, n)
+            )
+            ns_ref[r] = grown.astype(BF)
+    gain = gain_ref[...]
+    at = tr
+    out_rows = []
+    for t in range(steps):
+        y = ce[t * rows : (t + 1) * rows] * z[t * rows : (t + 1) * rows]
+        for s in range(t + 1):
+            y = y + ce[at : at + rows] * x[s]
+            at += rows
+        g = g_ref[t].astype(F32)
+        gated = y * (g / (1.0 + jnp.exp(-g)))
+        sq = gated * gated
+        part = sq[:, :LANES]
+        for b in range(1, cols // LANES):
+            part = part + sq[:, b * LANES : (b + 1) * LANES]
+        ss_ref[t * rows : (t + 1) * rows, :] += part
+        out_rows.append(gated * gain)
+    u_ref[:tr, pl.ds(pl.multiple_of(j * cols, cols), cols)] = jnp.concatenate(out_rows, axis=0).astype(BF)
+
+
+def state_call(args, part, parts, hb, carried=None):
+    (idx, store, state, x, g, lg, w, q, rate, skip, gain) = args
+    steps, rows, width = x.shape
+    heads = rate.shape[0]
+    tr = steps * rows
+    cols = hb * HEAD_WIDTH
+    n = w.shape[2]
+    grid = heads // hb // parts
+    first = part * grid
+    with_slots = part == 0
+    blocked = lambda j: (0, 0, first + j)
+    whole3 = lambda j: (0, 0, 0)
+    whole2 = lambda j: (0, 0)
+    state_spec = pl.BlockSpec((rows, hb, HEAD_WIDTH, n), lambda j: (0, first + j, 0, 0))
+    in_specs = [
+        pl.BlockSpec((steps, rows, cols), blocked),
+        pl.BlockSpec((steps, rows, cols), blocked),
+        pl.BlockSpec((steps, rows, heads), whole3),
+        pl.BlockSpec((1, heads), whole2),
+        pl.BlockSpec((1, heads), whole2),
+        pl.BlockSpec((1, cols), lambda j: (0, first + j)),
+        pl.BlockSpec((steps, rows, n), whole3),
+        pl.BlockSpec((steps, rows, n), whole3),
+        state_spec,
+    ]
+    operands = [x, g, lg, rate[None], skip[None], gain[None], w, q, state]
+    aliases = {}
+    if with_slots:
+        in_specs = [pl.BlockSpec(memory_space=pltpu.SMEM)] * 2 + in_specs
+        operands = [idx, store] + operands
+    else:
+        in_specs.append(pl.BlockSpec(memory_space=pl.ANY))
+        operands.append(carried)
+        aliases = {len(operands) - 1: 0}
+    u_rows = tr + (EXT if with_slots else 0)
+    u_cols = width // parts
+    coef_rows = (steps * (steps + 1) // 2 + 2 * steps) * rows
+    return pl.pallas_call(
+        functools.partial(state_body, first, with_slots, hb, steps, rows, heads),
+        grid=(grid,),
+        in_specs=in_specs,
+        out_specs=[
+            state_spec,
+            pl.BlockSpec((u_rows, u_cols), whole2),
+            pl.BlockSpec((tr, LANES), whole2),
+        ],
+        out_shape=[
+            jax.ShapeDtypeStruct(state.shape, BF),
+            jax.ShapeDtypeStruct((u_rows, u_cols), BF),
+            jax.ShapeDtypeStruct((tr, LANES), F32),
+        ],
+        scratch_shapes=[
+            pltpu.VMEM((coef_rows, heads), BF),
+            pltpu.VMEM((coef_rows, heads), BF),
+            pltpu.VMEM((rows // 2, tr, 2 * n), BF),
+            pltpu.VMEM((rows // 2, tr, 2 * n), BF),
+            pltpu.VMEM((rows, heads, LANES), F32),
+            pltpu.VMEM((tr, LANES), F32),
+        ],
+        input_output_aliases=aliases,
+        compiler_params=pltpu.CompilerParams(
+            dimension_semantics=("arbitrary",), vmem_limit_bytes=40 * 1024 * 1024
+        ),
+        cost_estimate=pl.CostEstimate(
+            flops=4 * tr * rows * heads * HEAD_WIDTH * n // parts,
+            bytes_accessed=4 * state.size // parts,
+            transcendentals=0,
+        ),
+        name=f"state_part{part}",
+    )(*operands)
+
+
+def base_body(per, count, order_ref, u1_ref, u2_ref, w_ref, *outs):
+    tr, half = u2_ref.shape
+    tile = dot(u1_ref[:tr], w_ref[:half]) + dot(u2_ref[...], w_ref[half:])
+    step = pl.program_id(0)
+    for k in range(count):
+
+        @pl.when(step // per == k)
+        def _():
+            outs[k][...] = tile.astype(outs[k].dtype)
+
+
+def base_call(u1, u2, weight, order, features, types, tile, name):
+    tr = u2.shape[0]
+    count = len(types)
+    per = features // tile
+    depth = weight.shape[0]
+
+    def out_map(k):
+        return lambda g, o: (0, jnp.clip(g - k * per, 0, per - 1))
+
+    return pl.pallas_call(
+        functools.partial(base_body, per, count),
+        grid_spec=pltpu.PrefetchScalarGridSpec(
+            num_scalar_prefetch=1,
+            grid=(count * per,),
+            in_specs=[
+                pl.BlockSpec(u1.shape, lambda g, o: (0, 0)),
+                pl.BlockSpec(u2.shape, lambda g, o: (0, 0)),
+                pl.BlockSpec((depth, tile), lambda g, o: (0, o[g // per] * per + g % per)),
+            ],
+            out_specs=[pl.BlockSpec((tr, tile), out_map(k)) for k in range(count)],
+        ),
+        out_shape=[jax.ShapeDtypeStruct((tr, features), t) for t in types],
+        compiler_params=pltpu.CompilerParams(
+            dimension_semantics=("arbitrary",), vmem_limit_bytes=24 * 1024 * 1024
+        ),
+        cost_estimate=pl.CostEstimate(
+            flops=2 * tr * depth * features * count,
+            bytes_accessed=2 * depth * features * count,
+            transcendentals=0,
+        ),
+        name=name,
+    )(order, u1, u2, weight)
+
+
+def slot_column(u1_ref, tr):
+    blocks = [u1_ref[tr : tr + EXT, b * LANES : b * LANES + LANES].astype(F32) for b in range(tr // EXT)]
+    return jnp.concatenate(blocks, axis=0)
+
+
+def down_body(sources, rank, *refs):
+    first_ref = refs[0]
+    u1s = refs[1 : 1 + sources]
+    u2s = refs[1 + sources : 1 + 2 * sources]
+    down_ref, ssa_ref, ssb_ref, msg_ref, acc_ref = refs[1 + 2 * sources :]
+    tr, half = u2s[0].shape
+    g = pl.program_id(0)
+    tile = down_ref.shape[0]
+    base = first_ref[0] + g * (tile // rank)
+    cell = (lax.broadcasted_iota(jnp.int32, (tr, tile), 1) // rank + base).astype(F32)
+    for k in range(sources):
+        part = dot(u1s[k][:tr], down_ref[:, :half], NT) + dot(u2s[k][...], down_ref[:, half:], NT)
+        slot = slot_column(u1s[k], tr)
+        slot = jnp.concatenate([slot] * (tile // LANES), axis=1)
+        part = jnp.where(cell == slot, part, 0.0)
+        total = part[:, :LANES]
+        for b in range(1, tile // LANES):
+            total = total + part[:, b * LANES : (b + 1) * LANES]
+
+        @pl.when(g == 0)
+        def _():
+            acc_ref[k] = total
+
+        @pl.when(g > 0)
+        def _():
+            acc_ref[k] += total
+
+    @pl.when(g == pl.num_programs(0) - 1)
+    def _():
+        lane = lax.broadcasted_iota(jnp.int32, (tr, LANES), 1)
+        for k in range(0, sources, 2):
+            a, b = acc_ref[k], acc_ref[k + 1]
+            a = a + pltpu.roll(a, rank, 1)
+            b = b + pltpu.roll(b, rank, 1)
+            at = k // 2 * tr
+            msg_ref[at : at + tr, :] = jnp.where(lane < rank, a, b).astype(BF)
+        ss = jnp.sum(ssa_ref[...] + ssb_ref[...], axis=1, keepdims=True)
+        ss = jnp.broadcast_to(ss, (tr, LANES))
+        hi = ss.astype(BF).astype(F32)
+        lo = ss - hi
+        lane = lax.broadcasted_iota(jnp.int32, (EXT, LANES), 1)
+        row = jnp.zeros((EXT, LANES), F32)
+        for b in range(tr // EXT):
+            piece = slice(b * EXT, (b + 1) * EXT)
+            row = jnp.where(lane == 2 * b, hi[piece], row)
+            row = jnp.where(lane == 2 * b + 1, lo[piece], row)
+        msg_ref[sources // 2 * tr :, :] = row.astype(BF)
+
+
+def down_call(first, u1s, u2s, down, rank, ssa, ssb, tile=256):
+    tr = u2s[0].shape[0]
+    sources = len(u1s)
+    wide, depth = down.shape
+    whole = lambda a: pl.BlockSpec(a.shape, lambda g: (0, 0))
+    return pl.pallas_call(
+        functools.partial(down_body, sources, rank),
+        grid=(wide // tile,),
+        in_specs=[pl.BlockSpec(memory_space=pltpu.SMEM)]
+        + [whole(a) for a in u1s]
+        + [whole(a) for a in u2s]
+        + [pl.BlockSpec((tile, depth), lambda g: (g, 0)), whole(ssa), whole(ssb)],
+        out_specs=pl.BlockSpec((sources // 2 * tr + EXT, LANES), lambda g: (0, 0)),
+        out_shape=jax.ShapeDtypeStruct((sources // 2 * tr + EXT, LANES), BF),
+        scratch_shapes=[pltpu.VMEM((sources, tr, LANES), F32)],
+        compiler_params=pltpu.CompilerParams(
+            dimension_semantics=("arbitrary",), vmem_limit_bytes=24 * 1024 * 1024
+        ),
+        cost_estimate=pl.CostEstimate(
+            flops=2 * sources * tr * wide * depth, bytes_accessed=2 * wide * depth, transcendentals=0
+        ),
+        name="adapter_down",
+    )(first, *u1s, *u2s, down, ssa, ssb)
+
+
+def up_body(sources, rank, width, nmsg, *refs):
+    first_ref = refs[0]
+    msgs = refs[1 : 1 + nmsg]
+    u1s = refs[1 + nmsg : 1 + nmsg + sources]
+    up_ref, here_ref, side_ref, far_ref, scale_ref, lhs_ref = refs[1 + nmsg + sources :]
+    tr = here_ref.shape[0]
+    wide = up_ref.shape[0]
+    g = pl.program_id(0)
+
+    @pl.when(g == 0)
+    def _():
+        total = msgs[0][...].astype(F32)
+        for m in msgs[1:]:
+            total = total + m[...].astype(F32)
+        lane = lax.broadcasted_iota(jnp.int32, (tr, LANES), 1)
+        cell = (lax.broadcasted_iota(jnp.int32, (tr, wide), 1) // rank + first_ref[0]).astype(F32)
+        for k in range(sources):
+            at = k // 2 * tr
+            v = total[at : at + tr]
+            turned = pltpu.roll(v, rank, 1)
+            v = jnp.where((lane < rank) == (k % 2 == 0), v, turned)
+            v = jnp.concatenate([v] * (wide // LANES), axis=1)
+            slot = jnp.concatenate([slot_column(u1s[k], tr)] * (wide // LANES), axis=1)
+            lhs_ref[k] = jnp.where(cell == slot, v, 0.0).astype(BF)
+        tail = total[sources // 2 * tr :]
+        lane = lax.broadcasted_iota(jnp.int32, (EXT, LANES), 1)
+        for b in range(tr // EXT):
+            pick = (lane == 2 * b) | (lane == 2 * b + 1)
+            ss = jnp.sum(jnp.where(pick, tail, 0.0), axis=1, keepdims=True)
+            scale = lax.rsqrt(ss / width + EPSILON)
+            scale_ref[b * EXT : (b + 1) * EXT, :] = jnp.broadcast_to(scale, (EXT, LANES))
+
+    here_ref[...] = dot(lhs_ref[0], up_ref[...]).astype(BF)
+    side_ref[:tr] = dot(lhs_ref[1], up_ref[...]).astype(BF)
+    side_ref[tr:] = dot(lhs_ref[3], up_ref[...]).astype(BF)
+    far_ref[...] = dot(lhs_ref[2], up_ref[...]).astype(BF)
+
+
+def up_call(first, msgs, u1s, up, rank, width, tr, tile=256):
+    sources = len(u1s)
+    wide, features = up.shape
+    whole = lambda a: pl.BlockSpec(a.shape, lambda g: (0, 0))
+    cut = lambda r: pl.BlockSpec((r, tile), lambda g: (0, g))
+    return pl.pallas_call(
+        functools.partial(up_body, sources, rank, width, len(msgs)),
+        grid=(features // tile,),
+        in_specs=[pl.BlockSpec(memory_space=pltpu.SMEM)]
+        + [whole(a) for a in msgs]
+        + [whole(a) for a in u1s]
+        + [pl.BlockSpec((wide, tile), lambda g: (0, g))],
+        out_specs=[cut(tr), cut(2 * tr), cut(tr), pl.BlockSpec((tr, LANES), lambda g: (0, 0))],
+        out_shape=[
+            jax.ShapeDtypeStruct((tr, features), BF),
+            jax.ShapeDtypeStruct((2 * tr, features), BF),
+            jax.ShapeDtypeStruct((tr, features), BF),
+            jax.ShapeDtypeStruct((tr, LANES), F32),
+        ],
+        scratch_shapes=[pltpu.VMEM((sources, tr, wide), BF)],
+        compiler_params=pltpu.CompilerParams(
+            dimension_semantics=("arbitrary",), vmem_limit_bytes=24 * 1024 * 1024
+        ),
+        cost_estimate=pl.CostEstimate(
+            flops=2 * sources * tr * wide * features, bytes_accessed=2 * wide * features, transcendentals=0
+        ),
+        name="adapter_up",
+    )(first, *msgs, *u1s, up)
+
+
+def swap(a, axis, size, bit):
+    return lax.ppermute(a, axis, [(i, i ^ bit) for i in range(size)])
+
+
+def per_device_pairs(
+    dp,
+    tensor,
+    row_adapter_index,
+    adapter_storage_row,
+    initial_head_state,
+    step_head_input,
+    step_gate_input,
+    step_size_logits,
+    state_write_key,
+    state_read_query,
+    head_decay_rate,
+    head_skip_gain,
+    gated_norm_gain,
+    output_weight,
+    adapter_down_weight,
+    adapter_up_weight,
+):
+    steps, rows, width = step_head_input.shape
+    tr = steps * rows
+    stored, _, rank = adapter_down_weight.shape
+    features = adapter_up_weight.shape[2]
+    down = jnp.swapaxes(adapter_down_weight, 1, 2).reshape(stored * rank, width)
+    up = adapter_up_weight.reshape(stored * rank, features)
+    me = lax.axis_index("tensor")
+    first = (lax.axis_index("dp") * stored)[None].astype(jnp.int32)
+
+    state_args = (
+        row_adapter_index,
+        adapter_storage_row,
+        initial_head_state,
+        step_head_input,
+        step_gate_input,
+        step_size_logits,
+        state_write_key,
+        state_read_query,
+        head_decay_rate,
+        head_skip_gain,
+        gated_norm_gain,
+    )
+    hb = 4
+    carried, u1, ssa = state_call(state_args, 0, 2, hb)
+    x1 = swap(u1, "dp", dp, 2)
+    carried, u2, ssb = state_call(state_args, 1, 2, hb, carried)
+    x2 = swap(u2, "dp", dp, 2)
+    c1 = swap(u1, "dp", dp, 1)
+    c2 = swap(u2, "dp", dp, 1)
+
+    order = (me ^ jnp.array([3, 2, 1, 0], jnp.int32)).astype(jnp.int32)
+    (far,) = base_call(u1, u2, output_weight, order[:1], features, [BF], 512, "base_first")
+    near_in = swap(far, "tensor", tensor, 1)
+    mid, near, own = base_call(u1, u2, output_weight, order[1:], features, [F32, BF, F32], 512, "base_rest")
+    near_own = swap(near, "tensor", tensor, 1)
+    mid_in = swap((mid + near_in.astype(F32)).astype(BF), "tensor", tensor, 2)
+
+    d1 = swap(x1, "dp", dp, 1)
+    d2 = swap(x2, "dp", dp, 1)
+    u1s = [u1, c1, x1, d1]
+    u2s = [u2, c2, x2, d2]
+    msg = down_call(first, u1s, u2s, down, rank, ssa, ssb)
+    msgs = [msg] + [swap(msg, "tensor", tensor, k) for k in range(1, tensor)]
+    here, side, over, scale = up_call(first, msgs, u1s, up, rank, width * tensor, tr)
+    side_in = swap(side, "dp", dp, 1)
+    over_in = swap(over + side_in[tr:], "dp", dp, 2)
+    total = own + near_own.astype(F32) + mid_in.astype(F32)
+    total = total + here.astype(F32) + side_in[:tr].astype(F32) + over_in.astype(F32)
+    mixed_out = (total * scale[:, :1]).astype(BF).reshape(steps, rows, features)
+    return mixed_out, carried
 
 
 def slot_lookup(row_adapter_index, adapter_storage_row):
@@ -17,7 +480,7 @@
     return jnp.sum(jnp.where(match, adapter_storage_row[None, :], 0), axis=1)
 
 
-def per_device(
+def per_device_any(
     row_adapter_index,
     adapter_storage_row,
     initial_head_state,
@@ -113,8 +576,12 @@
         P("dp", "tensor", None),
         P("dp", None, "tensor"),
     )
+    dp, tensor = mesh.shape["dp"], mesh.shape["tensor"]
+    body = per_device_any
+    if dp == 4 and tensor == 4:
+        body = functools.partial(per_device_pairs, dp, tensor)
     return jax.shard_map(
-        per_device,
+        body,
         mesh=mesh,
         in_specs=placed,
         out_specs=(P(None, ("groups", "dp"), "tensor"), P(("groups", "dp"), "tensor", None, None)),

time: 183 us -> 93.4 us (0.51)
  other arithmetic: 73.1 us -> 0.95 us
  blocking collectives: 44.1 us -> 0 us
  Pallas kernels: 0 us -> 37.7 us
  local copies, waits for them, and re-layouts: 3.98 us -> 24.9 us
  matrix products: 17.4 us -> 0 us
  between operations: 15.6 us -> 0.77 us
  waiting for transfers between devices: 28.9 us -> 14.9 us
  starting transfers between devices: 0.13 us -> 13.6 us
    reduce_sum x3 -> x0, other arithmetic: 62.5 us -> none  [the longest x1 62.2 us: per_device(): jnp.sum(updated * reader[:, None, None, :], axis=3)]
    psum x2 -> x0, blocking collectives: 38.8 us -> none  [the longest x1 25.3 us: per_device(): down_projected = lax.psum(picked, 'tensor').astype(jnp.bfloat16)]
    pallas_call x0 -> x6, Pallas kernels: none -> 37.7 us  [the longest x2 16.3 us: state_call(): pl.pallas_call(functools.partial(state_body, first, with_slots, hb, steps...]
    reduce_scatter x2 -> x0, waiting for transfers between devices: 26.7 us -> none  [the longest x1 26.7 us: per_device(): lax.psum_scatter(adapter_delta, 'dp', scatter_dimension=1, tiled=True)]
    unnamed x11 -> x44, local copies, waits for them, and re-layouts: 0.1 us -> 24.7 us
    dot_general x3 -> x0, matrix products: 17.4 us -> none  [the longest x1 10.2 us: per_device(): jnp.dot(normed.reshape(steps_n * row_count, width), output_weight, prefer...]
    ppermute x0 -> x14, waiting for transfers between devices: none -> 14.9 us  [swap(): return lax.ppermute(a, axis, [(i, i ^ bit) for i in range(size)])]
    ppermute x0 -> x14, starting transfers between devices: none -> 13.6 us  [swap(): return lax.ppermute(a, axis, [(i, i ^ bit) for i in range(size)])]
  transfers between devices with their start and end apart: 3 -> 14, of which waited for: 2 -> 3; matrix products, arithmetic and copies ran while one was open for 10% -> 0% of each run, Pallas kernels for 0% -> 18%
where the time goes in v1:
time: 93.4 us; the launch traced here: 92.8 us
  Pallas kernels  37.7 us (40%)
  local copies, waits for them, and re-layouts  24.9 us (27%)
  waiting for transfers between devices  14.9 us (16%)
  starting transfers between devices  13.6 us (15%)
  other arithmetic  0.95 us (1%)
    unnamed x44, local copies, waits for them, and re-layouts  24.7 us
    pallas_call x2, Pallas kernels, state_call(): pl.pallas_call(functools.partial(state_body, first, with_slots, hb, steps...  16.3 us
    ppermute x14, waiting for transfers between devices, swap(): return lax.ppermute(a, axis, [(i, i ^ bit) for i in range(size)])  14.9 us
    ppermute x14, starting transfers between devices, swap(): return lax.ppermute(a, axis, [(i, i ^ bit) for i in range(size)])  13.6 us
    pallas_call x1, Pallas kernels, down_call(): pl.pallas_call(functools.partial(down_body, sources, rank), grid=(wide //...  12.5 us
    pallas_call x2, Pallas kernels, base_call(): pl.pallas_call(functools.partial(base_body, per, count), grid_spec=pltpu....  6.32 us
    pallas_call x1, Pallas kernels, up_call(): pl.pallas_call(functools.partial(up_body, sources, rank, width, len(msgs)...  2.57 us
  transfers between devices with their start and end apart: 14, of which 3 were waited for; matrix products, arithmetic and copies ran while one was open for 0% of the time, Pallas kernels for 18%

profile of v1, /device:TPU:0, one launch (start us, length us, event | category | flops | bytes accessed | tf_op | source)
XLA Modules:
  0.0 92.8 jit_solution(18088344613324220962)
XLA Ops:
  0.6 4.6 %copy-done.2 = bf16[24,32,64,128]{3,2,1,0:T(8,128)(2,1)S(1)} copy-done((bf16[24,32,64,128]{3,2,1,0:T(8,128)(2,1)S(1)}, bf16[24,32,64,128]{3,2,1,0:T(8,128)(2,1)}, u32[]{:S(2)}) %copy-start.2) | copy-done | bytes 12582936
  5.2 1.0 %copy-done.6 = bf16[4,24,2048]{2,1,0:T(8,128)(2,1)S(1)} copy-done((bf16[4,24,2048]{2,1,0:T(8,128)(2,1)S(1)}, bf16[4,24,2048]{2,1,0:T(8,128)(2,1)}, u32[]{:S(2)}) %copy-start.6) | copy-done | bytes 393240
  6.2 1.0 %copy-done.8 = bf16[4,24,2048]{2,1,0:T(8,128)(2,1)S(1)} copy-done((bf16[4,24,2048]{2,1,0:T(8,128)(2,1)S(1)}, bf16[4,24,2048]{2,1,0:T(8,128)(2,1)}, u32[]{:S(2)}) %copy-start.8) | copy-done | bytes 393240
  7.2 0.8 copy-done.10
  8.0 0.7 copy-done.12
  12.8 8.4 %state_part0.1 = (bf16[24,32,64,128]{3,2,1,0:T(8,128)(2,1)}, bf16[112,1024]{1,0:T(8,128)(2,1)S(1)}, f32[96,128]{1,0:T(8,128)S(1)}) custom-call(s32[24]{0:T(128)S(1)} %copy-done.19, s32[64]{0:T(128)S(1)} %copy-done.20, bf16[4,24,2048]{2,1,0:T(8,128)(2,1)S(1)} %copy-done.6, bf16[4,24,2048]{2,1,0:T(8,128)(2,1)S(1)} %copy-done.8, f32[4,24,32]{2,1,0:T(8,128)S(1)} %copy-done.10, ...), custom_call_target="tpu_custom_call" | custom-call | flops 1207959552 | bytes 12582912 | tf_op jit(solution)/shard_map/state_part0/pallas_call | solution.py:175
  21.2 2.9 %collective-permute-start.4 = (bf16[112,1024]{1,0:T(8,128)(2,1)S(1)}, bf16[112,1024]{1,0:T(8,128)(2,1)S(1)}, u32[]{:S(2)}, u32[]{:S(2)}) collective-permute-start(bf16[112,1024]{1,0:T(8,128)(2,1)S(1)} %get-tuple-element.15.u1_ref.refs_1_.refs_5_), channel_id=1, source_target_pairs={{0,8},{4,12},{8,0},{12,4},{1,9},{5,13},{9,1},{13,5},{2,10},{6,14},... | collective-permute-start | bytes 688136 | tf_op jit(solution)/shard_map/ppermute | solution.py:403
  24.2 4.6 %copy-done.3 = bf16[24,32,64,128]{3,2,1,0:T(8,128)(2,1)S(1)} copy-done((bf16[24,32,64,128]{3,2,1,0:T(8,128)(2,1)S(1)}, bf16[24,32,64,128]{3,2,1,0:T(8,128)(2,1)}, u32[]{:S(2)}) %copy-start.3) | copy-done | bytes 12582936
  28.8 7.9 %state_part1.1 = (bf16[24,32,64,128]{3,2,1,0:T(8,128)(2,1)}, bf16[96,1024]{1,0:T(8,128)(2,1)S(1)}, f32[96,128]{1,0:T(8,128)S(1)}) custom-call(bf16[4,24,2048]{2,1,0:T(8,128)(2,1)S(1)} %copy-done.7, bf16[4,24,2048]{2,1,0:T(8,128)(2,1)S(1)} %copy-done.9, f32[4,24,32]{2,1,0:T(8,128)S(1)} %copy-done.11, ...), custom_call_target="tpu_custom_call", output_to_operand_aliasing={{0}: (9, {})} | custom-call | flops 1207959552 | bytes 12582912 | tf_op jit(solution)/shard_map/state_part1/pallas_call | solution.py:175
  37.3 5.8 %collective-permute-done.7.refs_7_ = bf16[96,1024]{1,0:T(8,128)(2,1)S(1)} collective-permute-done((bf16[96,1024]{1,0:T(8,128)(2,1)S(1)}, bf16[96,1024]{1,0:T(8,128)(2,1)S(1)}, u32[]{:S(2)}, u32[]{:S(2)}) %collective-permute-start.7) | collective-permute-done | bytes 196640 | tf_op jit(solution)/shard_map/ppermute | solution.py:403
  43.1 1.6 %collective-permute-done.8.refs_8_ = bf16[96,1024]{1,0:T(8,128)(2,1)} collective-permute-done((bf16[96,1024]{1,0:T(8,128)(2,1)S(1)}, bf16[96,1024]{1,0:T(8,128)(2,1)}, u32[]{:S(2)}, u32[]{:S(2)}) %collective-permute-start.8) | collective-permute-done | bytes 196640 | tf_op jit(solution)/shard_map/ppermute | solution.py:403
  44.7 2.2 %copy-done.4 = bf16[16,2048,64]{1,2,0:T(8,128)(2,1)S(1)} copy-done((bf16[16,2048,64]{1,2,0:T(8,128)(2,1)S(1)}, bf16[16,2048,64]{1,2,0:T(8,128)(2,1)}, u32[]{:S(2)}) %copy-start.4) | copy-done | bytes 4194328
  46.8 12.5 %adapter_down.1.refs_1_ = bf16[208,128]{1,0:T(8,128)(2,1)S(1)} custom-call(s32[1]{0:T(128)} %bitcast.3.refs_0_, bf16[112,1024]{1,0:T(8,128)(2,1)S(1)} %get-tuple-element.15.u1_ref.refs_1_.refs_5_, bf16[112,1024]{1,0:T(8,128)(2,1)S(1)} %collective-permute-done.3.refs_2_.refs_6_, bf16[112,1024]{1,0:T(8,128)(2,1)S(1)} %collective-permute-done.4.refs_3_.refs_7_, ...), custom_call_target="tpu_custom_call" | custom-call | flops 1610612736 | bytes 4194304 | tf_op jit(solution)/shard_map/adapter_down/pallas_call | solution.py:314
  59.3 2.7 %collective-permute-start.10 = (bf16[208,128]{1,0:T(8,128)(2,1)S(1)}, bf16[208,128]{1,0:T(8,128)(2,1)S(1)}, u32[]{:S(2)}, u32[]{:S(2)}) collective-permute-start(bf16[208,128]{1,0:T(8,128)(2,1)S(1)} %adapter_down.1.refs_1_), channel_id=1, source_target_pairs={{0,2},{1,3},{2,0},{3,1},{4,6},{5,7},{6,4},{7,5},{8,10},{9,11},{10,... | collective-permute-start | bytes 159752 | tf_op jit(solution)/shard_map/ppermute | solution.py:403
  62.0 1.3 %collective-permute-start.11 = (bf16[208,128]{1,0:T(8,128)(2,1)S(1)}, bf16[208,128]{1,0:T(8,128)(2,1)S(1)}, u32[]{:S(2)}, u32[]{:S(2)}) collective-permute-start(bf16[208,128]{1,0:T(8,128)(2,1)S(1)} %adapter_down.1.refs_1_), channel_id=1, source_target_pairs={{0,3},{1,2},{2,1},{3,0},{4,7},{5,6},{6,5},{7,4},{8,11},{9,10},{10,... | collective-permute-start | bytes 159752 | tf_op jit(solution)/shard_map/ppermute | solution.py:403
  63.6 5.8 %copy-done = bf16[2048,4096]{1,0:T(8,128)(2,1)S(1)} copy-done((bf16[2048,4096]{1,0:T(8,128)(2,1)S(1)}, bf16[2048,4096]{1,0:T(8,128)(2,1)}, u32[]{:S(2)}) %copy-start) | copy-done | bytes 16777240
  69.4 1.5 %base_first.1 = bf16[96,1024]{1,0:T(8,128)(2,1)S(1)} custom-call(s32[1]{0:T(128)S(1)} %bitcast.18, bf16[112,1024]{1,0:T(8,128)(2,1)S(1)} %get-tuple-element.15.u1_ref.refs_1_.refs_5_, bf16[96,1024]{1,0:T(8,128)(2,1)S(1)} %get-tuple-element.17.u2_ref.refs_5_, bf16[2048,4096]{1,0:T(8,128)(2,1)S(1)} %copy-done), custom_call_target="tpu_custom_call" | custom-call | flops 402653184 | bytes 4194304 | tf_op jit(solution)/shard_map/base_first/pallas_call | solution.py:230
  70.8 1.9 %collective-permute-start.1 = (bf16[96,1024]{1,0:T(8,128)(2,1)S(1)}, bf16[96,1024]{1,0:T(8,128)(2,1)S(1)}, u32[]{:S(2)}, u32[]{:S(2)}) collective-permute-start(bf16[96,1024]{1,0:T(8,128)(2,1)S(1)} %base_first.1), channel_id=1, source_target_pairs={{0,1},{1,0},{2,3},{3,2},{4,5},{5,4},{6,7},{7,6},{8,9},{9,8},{10,11... | collective-permute-start | bytes 589832 | tf_op jit(solution)/shard_map/ppermute | solution.py:403
  72.7 2.6 %adapter_up.1 = (bf16[96,1024]{1,0:T(8,128)(2,1)S(1)}, bf16[192,1024]{1,0:T(8,128)(2,1)S(1)}, bf16[96,1024]{1,0:T(8,128)(2,1)S(1)}, f32[96,128]{1,0:T(8,128)S(1)}) custom-call(s32[1]{0:T(128)} %bitcast.3.refs_0_, bf16[208,128]{1,0:T(8,128)(2,1)S(1)} %adapter_down.1.refs_1_, bf16[208,128]{1,0:T(8,128)(2,1)S(1)} %collective-permute-done.9.refs_2_, ...), custom_call_target="tpu_custom_call" | custom-call | flops 805306368 | bytes 2097152 | tf_op jit(solution)/shard_map/adapter_up/pallas_call | solution.py:377
  75.5 4.9 %base_rest.1 = (f32[96,1024]{1,0:T(8,128)S(1)}, bf16[96,1024]{1,0:T(8,128)(2,1)S(1)}, f32[96,1024]{1,0:T(8,128)S(1)}) custom-call(s32[3]{0:T(128)S(1)} %slice.15.order_ref, bf16[112,1024]{1,0:T(8,128)(2,1)S(1)} %get-tuple-element.15.u1_ref.refs_1_.refs_5_, bf16[96,1024]{1,0:T(8,128)(2,1)S(1)} %get-tuple-element.17.u2_ref.refs_5_, ...), custom_call_target="tpu_custom_call" | custom-call | flops 1207959552 | bytes 12582912 | tf_op jit(solution)/shard_map/base_rest/pallas_call | solution.py:230
  80.3 1.6 %collective-permute-start = (bf16[96,1024]{1,0:T(8,128)(2,1)S(1)}, bf16[96,1024]{1,0:T(8,128)(2,1)S(1)}, u32[]{:S(2)}, u32[]{:S(2)}) collective-permute-start(bf16[96,1024]{1,0:T(8,128)(2,1)S(1)} %get-tuple-element.19), channel_id=1, source_target_pairs={{0,1},{1,0},{2,3},{3,2},{4,5},{5,4},{6,7},{7,6},{8,9},{9,8},{10,11... | collective-permute-start | bytes 589832 | tf_op jit(solution)/shard_map/ppermute | solution.py:403
  82.0 1.8 %collective-permute-start.2 = (bf16[96,1024]{1,0:T(8,128)(2,1)S(1)}, bf16[96,1024]{1,0:T(8,128)(2,1)S(1)}, u32[]{:S(2)}, u32[]{:S(2)}) collective-permute-start(bf16[96,1024]{1,0:T(8,128)(2,1)S(1)} %add_convert_fusion), channel_id=1, source_target_pairs={{0,2},{1,3},{2,0},{3,1},{4,6},{5,7},{6,4},{7,5},{8,10},{9,11},{10,... | collective-permute-start | bytes 589832 | tf_op jit(solution)/shard_map/ppermute | solution.py:403
  84.4 7.5 %collective-permute-done = bf16[96,1024]{1,0:T(8,128)(2,1)S(1)} collective-permute-done((bf16[96,1024]{1,0:T(8,128)(2,1)S(1)}, bf16[96,1024]{1,0:T(8,128)(2,1)S(1)}, u32[]{:S(2)}, u32[]{:S(2)}) %collective-permute-start) | collective-permute-done | bytes 196640 | tf_op jit(solution)/shard_map/ppermute | solution.py:403
  91.9 0.9 multiply_convert_fusion
  (60 shorter events, 5.8 us)
Async XLA Ops:
  12.8 11.4 %copy-start.7 = (bf16[4,24,2048]{2,1,0:T(8,128)(2,1)S(1)}, bf16[4,24,2048]{2,1,0:T(8,128)(2,1)}, u32[]{:S(2)}) copy-start(bf16[4,24,2048]{2,1,0:T(8,128)(2,1)} %refs_0_.3) | copy-start | bytes 1179652
  12.8 11.4 %copy-start.9 = (bf16[4,24,2048]{2,1,0:T(8,128)(2,1)S(1)}, bf16[4,24,2048]{2,1,0:T(8,128)(2,1)}, u32[]{:S(2)}) copy-start(bf16[4,24,2048]{2,1,0:T(8,128)(2,1)} %refs_1_.3) | copy-start | bytes 1179652
  12.8 11.4 %copy-start.11 = (f32[4,24,32]{2,1,0:T(8,128)S(1)}, f32[4,24,32]{2,1,0:T(8,128)}, u32[]{:S(2)}) copy-start(f32[4,24,32]{2,1,0:T(8,128)} %refs_2_.3) | copy-start | bytes 36868
  12.8 11.4 %copy-start.13 = (bf16[4,24,128]{2,1,0:T(8,128)(2,1)S(1)}, bf16[4,24,128]{2,1,0:T(8,128)(2,1)}, u32[]{:S(2)}) copy-start(bf16[4,24,128]{2,1,0:T(8,128)(2,1)} %refs_6_.1) | copy-start | bytes 73732
  12.8 11.4 %copy-start.15 = (bf16[4,24,128]{2,1,0:T(8,128)(2,1)S(1)}, bf16[4,24,128]{2,1,0:T(8,128)(2,1)}, u32[]{:S(2)}) copy-start(bf16[4,24,128]{2,1,0:T(8,128)(2,1)} %refs_7_.1) | copy-start | bytes 73732
  21.2 15.5 %collective-permute-start.4 = (bf16[112,1024]{1,0:T(8,128)(2,1)S(1)}, bf16[112,1024]{1,0:T(8,128)(2,1)S(1)}, u32[]{:S(2)}, u32[]{:S(2)}) collective-permute-start(bf16[112,1024]{1,0:T(8,128)(2,1)S(1)} %get-tuple-element.15.u1_ref.refs_1_.refs_5_), channel_id=1, source_target_pairs={{0,8},{4,12},{8,0},{12,4},{1,9},{5,13},{9,1},{13,5},{2,10},{6,14},... | collective-permute-start | bytes 688136 | tf_op jit(solution)/shard_map/ppermute | solution.py:403
  24.2 4.6 %copy-start.3 = (bf16[24,32,64,128]{3,2,1,0:T(8,128)(2,1)S(1)}, bf16[24,32,64,128]{3,2,1,0:T(8,128)(2,1)}, u32[]{:S(2)}) copy-start(bf16[24,32,64,128]{3,2,1,0:T(8,128)(2,1)} %refs_8_.3) | copy-start | bytes 37748740
  28.8 34.8 %copy-start.21 = (s32[4]{0:T(128)S(1)}, s32[4]{0:T(128)}, u32[]{:S(2)}) copy-start(s32[4]{0:T(128)} %constant.11.clone) | copy-start | bytes 52
  28.8 43.9 %copy-start.5 = (bf16[16,64,1024]{2,1,0:T(8,128)(2,1)S(1)}, bf16[16,64,1024]{2,1,0:T(8,128)(2,1)}, u32[]{:S(2)}) copy-start(bf16[16,64,1024]{2,1,0:T(8,128)(2,1)} %param.28) | copy-start | bytes 6291460
  36.7 6.4 %collective-permute-start.7 = (bf16[96,1024]{1,0:T(8,128)(2,1)S(1)}, bf16[96,1024]{1,0:T(8,128)(2,1)S(1)}, u32[]{:S(2)}, u32[]{:S(2)}) collective-permute-start(bf16[96,1024]{1,0:T(8,128)(2,1)S(1)} %get-tuple-element.17.u2_ref.refs_5_), channel_id=1, source_target_pairs={{0,8},{4,12},{8,0},{12,4},{1,9},{5,13},{9,1},{13,5},{2,10},{6,14},... | collective-permute-start | bytes 589832 | tf_op jit(solution)/shard_map/ppermute | solution.py:403
  36.7 6.4 %collective-permute-start.3 = (bf16[112,1024]{1,0:T(8,128)(2,1)S(1)}, bf16[112,1024]{1,0:T(8,128)(2,1)S(1)}, u32[]{:S(2)}, u32[]{:S(2)}) collective-permute-start(bf16[112,1024]{1,0:T(8,128)(2,1)S(1)} %get-tuple-element.15.u1_ref.refs_1_.refs_5_), channel_id=1, source_target_pairs={{0,4},{4,0},{8,12},{12,8},{1,5},{5,1},{9,13},{13,9},{2,6},{6,2},{1... | collective-permute-start | bytes 688136 | tf_op jit(solution)/shard_map/ppermute | solution.py:403
  36.7 7.9 %collective-permute-start.5 = (bf16[112,1024]{1,0:T(8,128)(2,1)S(1)}, bf16[112,1024]{1,0:T(8,128)(2,1)S(1)}, u32[]{:S(2)}, u32[]{:S(2)}) collective-permute-start(bf16[112,1024]{1,0:T(8,128)(2,1)S(1)} %collective-permute-done.4.refs_3_.refs_7_), channel_id=1, source_target_pairs={{0,4},{4,0},{8,12},{12,8},{1,5},{5,1},{9,13},{13,9},{2,6},{6,2},{1... | collective-permute-start | bytes 688136 | tf_op jit(solution)/shard_map/ppermute | solution.py:403
  37.2 5.8 %collective-permute-start.6 = (bf16[96,1024]{1,0:T(8,128)(2,1)S(1)}, bf16[96,1024]{1,0:T(8,128)(2,1)}, u32[]{:S(2)}, u32[]{:S(2)}) collective-permute-start(bf16[96,1024]{1,0:T(8,128)(2,1)S(1)} %get-tuple-element.17.u2_ref.refs_5_), channel_id=1, source_target_pairs={{0,4},{4,0},{8,12},{12,8},{1,5},{5,1},{9,13},{13,9},{2,6},{6,2},{1... | collective-permute-start | bytes 589832 | tf_op jit(solution)/shard_map/ppermute | solution.py:403
  43.1 1.6 %collective-permute-start.8 = (bf16[96,1024]{1,0:T(8,128)(2,1)S(1)}, bf16[96,1024]{1,0:T(8,128)(2,1)}, u32[]{:S(2)}, u32[]{:S(2)}) collective-permute-start(bf16[96,1024]{1,0:T(8,128)(2,1)S(1)} %collective-permute-done.7.refs_7_), channel_id=1, source_target_pairs={{0,4},{4,0},{8,12},{12,8},{1,5},{5,1},{9,13},{13,9},{2,6},{6,2},{1... | collective-permute-start | bytes 589832 | tf_op jit(solution)/shard_map/ppermute | solution.py:403
  59.3 13.4 %collective-permute-start.10 = (bf16[208,128]{1,0:T(8,128)(2,1)S(1)}, bf16[208,128]{1,0:T(8,128)(2,1)S(1)}, u32[]{:S(2)}, u32[]{:S(2)}) collective-permute-start(bf16[208,128]{1,0:T(8,128)(2,1)S(1)} %adapter_down.1.refs_1_), channel_id=1, source_target_pairs={{0,2},{1,3},{2,0},{3,1},{4,6},{5,7},{6,4},{7,5},{8,10},{9,11},{10,... | collective-permute-start | bytes 159752 | tf_op jit(solution)/shard_map/ppermute | solution.py:403
  62.0 10.7 %collective-permute-start.11 = (bf16[208,128]{1,0:T(8,128)(2,1)S(1)}, bf16[208,128]{1,0:T(8,128)(2,1)S(1)}, u32[]{:S(2)}, u32[]{:S(2)}) collective-permute-start(bf16[208,128]{1,0:T(8,128)(2,1)S(1)} %adapter_down.1.refs_1_), channel_id=1, source_target_pairs={{0,3},{1,2},{2,1},{3,0},{4,7},{5,6},{6,5},{7,4},{8,11},{9,10},{10,... | collective-permute-start | bytes 159752 | tf_op jit(solution)/shard_map/ppermute | solution.py:403
  63.4 9.3 %collective-permute-start.9 = (bf16[208,128]{1,0:T(8,128)(2,1)S(1)}, bf16[208,128]{1,0:T(8,128)(2,1)S(1)}, u32[]{:S(2)}, u32[]{:S(2)}) collective-permute-start(bf16[208,128]{1,0:T(8,128)(2,1)S(1)} %adapter_down.1.refs_1_), channel_id=1, source_target_pairs={{0,1},{1,0},{2,3},{3,2},{4,5},{5,4},{6,7},{7,6},{8,9},{9,8},{10,11... | collective-permute-start | bytes 159752 | tf_op jit(solution)/shard_map/ppermute | solution.py:403
  63.6 5.8 %copy-start = (bf16[2048,4096]{1,0:T(8,128)(2,1)S(1)}, bf16[2048,4096]{1,0:T(8,128)(2,1)}, u32[]{:S(2)}) copy-start(bf16[2048,4096]{1,0:T(8,128)(2,1)} %w_ref.3) | copy-start | bytes 50331652
  69.4 6.1 %copy-start.1 = (bf16[2048,4096]{1,0:T(8,128)(2,1)S(1)}, bf16[2048,4096]{1,0:T(8,128)(2,1)}, u32[]{:S(2)}) copy-start(bf16[2048,4096]{1,0:T(8,128)(2,1)} %w_ref.3) | copy-start | bytes 50331652
  70.8 11.1 %collective-permute-start.1 = (bf16[96,1024]{1,0:T(8,128)(2,1)S(1)}, bf16[96,1024]{1,0:T(8,128)(2,1)S(1)}, u32[]{:S(2)}, u32[]{:S(2)}) collective-permute-start(bf16[96,1024]{1,0:T(8,128)(2,1)S(1)} %base_first.1), channel_id=1, source_target_pairs={{0,1},{1,0},{2,3},{3,2},{4,5},{5,4},{6,7},{7,6},{8,9},{9,8},{10,11... | collective-permute-start | bytes 589832 | tf_op jit(solution)/shard_map/ppermute | solution.py:403
  75.3 8.4 %collective-permute-start.12 = (bf16[192,1024]{1,0:T(8,128)(2,1)S(1)}, bf16[192,1024]{1,0:T(8,128)(2,1)S(1)}, u32[]{:S(2)}, u32[]{:S(2)}) collective-permute-start(bf16[192,1024]{1,0:T(8,128)(2,1)S(1)} %get-tuple-element.24), channel_id=1, source_target_pairs={{0,4},{4,0},{8,12},{12,8},{1,5},{5,1},{9,13},{13,9},{2,6},{6,2},{1... | collective-permute-start | bytes 1179656 | tf_op jit(solution)/shard_map/ppermute | solution.py:403
  80.3 11.6 %collective-permute-start = (bf16[96,1024]{1,0:T(8,128)(2,1)S(1)}, bf16[96,1024]{1,0:T(8,128)(2,1)S(1)}, u32[]{:S(2)}, u32[]{:S(2)}) collective-permute-start(bf16[96,1024]{1,0:T(8,128)(2,1)S(1)} %get-tuple-element.19), channel_id=1, source_target_pairs={{0,1},{1,0},{2,3},{3,2},{4,5},{5,4},{6,7},{7,6},{8,9},{9,8},{10,11... | collective-permute-start | bytes 589832 | tf_op jit(solution)/shard_map/ppermute | solution.py:403
  82.0 10.0 %collective-permute-start.2 = (bf16[96,1024]{1,0:T(8,128)(2,1)S(1)}, bf16[96,1024]{1,0:T(8,128)(2,1)S(1)}, u32[]{:S(2)}, u32[]{:S(2)}) collective-permute-start(bf16[96,1024]{1,0:T(8,128)(2,1)S(1)} %add_convert_fusion), channel_id=1, source_target_pairs={{0,2},{1,3},{2,0},{3,1},{4,6},{5,7},{6,4},{7,5},{8,10},{9,11},{10,... | collective-permute-start | bytes 589832 | tf_op jit(solution)/shard_map/ppermute | solution.py:403
  83.7 8.2 %collective-permute-start.13 = (bf16[96,1024]{1,0:T(8,128)(2,1)S(1)}, bf16[96,1024]{1,0:T(8,128)(2,1)S(1)}, u32[]{:S(2)}, u32[]{:S(2)}) collective-permute-start(bf16[96,1024]{1,0:T(8,128)(2,1)S(1)} %slice_add_fusion), channel_id=1, source_target_pairs={{0,8},{4,12},{8,0},{12,4},{1,9},{5,13},{9,1},{13,5},{2,10},{6,14},... | collective-permute-start | bytes 589832 | tf_op jit(solution)/shard_map/ppermute | solution.py:403
  (12 other events, 14.4 us)

commit v2 on v0

--- a/solution.py
+++ b/solution.py
@@ -1,13 +1,473 @@
+import functools
+
 import jax
 import jax.numpy as jnp
 from jax import lax
+from jax.experimental import pallas as pl
+from jax.experimental.pallas import tpu as pltpu
 from jax.sharding import PartitionSpec as P
 
 STATE_HEADS = 128
 HEAD_WIDTH = 64
-
-
 EPSILON = 1e-05
+
+BF = jnp.bfloat16
+F32 = jnp.float32
+NT = (((1,), (1,)), ((), ()))
+NN = (((1,), (0,)), ((), ()))
+LANES = 128
+EXT = 16
+MIB = 1024 * 1024
+
+VM = pl.BlockSpec(memory_space=pltpu.VMEM)
+ANY = pl.BlockSpec(memory_space=pl.ANY)
+
+
+def dot(a, b, dims=NN):
+    return lax.dot_general(a, b, dims, preferred_element_type=F32)
+
+
+def hbm(a):
+    return pltpu.with_memory_space_constraint(a, pltpu.HBM)
+
+
+def params(mib):
+    return pltpu.CompilerParams(vmem_limit_bytes=mib * MIB)
+
+
+def state_body(hb, *refs):
+    small_src = refs[:8]
+    s_ref, idx_ref, store_ref = refs[8:11]
+    ns_ref, u_ref, ss_ref = refs[11:14]
+    x_ref, g_ref, lg_ref, rate_ref, skip_ref, gain_ref, w_ref, q_ref = refs[14:22]
+    s_buf, o_buf, chi_ref, clo_ref, wbd_ref, qbd_ref, k4_ref, xet_ref, z_ref, sq_ref = refs[22:32]
+    small_sem, in_sem, out_sem, idx_buf, store_buf = refs[32:]
+    steps, rows, width = x_ref.shape
+    heads = lg_ref.shape[2]
+    n = w_ref.shape[2]
+    tr = steps * rows
+    cols = hb * HEAD_WIDTH
+    pairs = rows // 2
+    chunks = heads // hb
+
+    def state_in(c):
+        return pltpu.make_async_copy(
+            s_ref.at[:, pl.ds(c * hb, hb)], s_buf.at[:, pl.ds(c * hb, hb)], in_sem.at[c]
+        )
+
+    def state_out(c):
+        return pltpu.make_async_copy(
+            o_buf.at[:, pl.ds(c * hb, hb)], ns_ref.at[:, pl.ds(c * hb, hb)], out_sem.at[c]
+        )
+
+    small_dst = [x_ref, g_ref, lg_ref, rate_ref, skip_ref, gain_ref, w_ref, q_ref, idx_buf, store_buf]
+    small_src = list(small_src) + [idx_ref, store_ref]
+    copies = [
+        pltpu.make_async_copy(a, b, small_sem.at[i]) for i, (a, b) in enumerate(zip(small_src, small_dst))
+    ]
+    for i in (2, 3, 4, 6, 7, 0):
+        copies[i].start()
+    state_in(0).start()
+    for i in (1, 5, 8, 9):
+        copies[i].start()
+    for c in range(1, chunks):
+        state_in(c).start()
+    for i in (2, 3, 4, 6, 7):
+        copies[i].wait()
+
+    delta = [jax.nn.softplus(lg_ref[t]) for t in range(steps)]
+    keep = [jnp.exp(-delta[t] * rate_ref[...]) for t in range(steps)]
+    w = [w_ref[t].astype(F32) for t in range(steps)]
+    q = [q_ref[t].astype(F32) for t in range(steps)]
+    cum = []
+    for t in range(steps):
+        cum.append(keep[t] if t == 0 else cum[-1] * keep[t])
+    coef = list(cum)
+    cur = []
+    for t in range(steps):
+        cur = [v * keep[t] for v in cur] + [delta[t]]
+        for s in range(t + 1):
+            a = cur[s] * jnp.sum(w[s] * q[t], axis=1, keepdims=True)
+            if s == t:
+                a = a + skip_ref[...]
+            coef.append(a)
+    coef = jnp.concatenate(cur + coef, axis=0)
+    hi = coef.astype(BF)
+    chi_ref[...] = hi
+    clo_ref[...] = (coef - hi.astype(F32)).astype(BF)
+    eye = lax.broadcasted_iota(jnp.int32, (heads, heads), 0) == lax.broadcasted_iota(
+        jnp.int32, (heads, heads), 1
+    )
+    for r in range(rows):
+        col = jnp.sum(jnp.where(eye, cum[-1][r : r + 1, :], 0.0), axis=1, keepdims=True)
+        k4_ref[r] = jnp.broadcast_to(col, (heads, LANES))
+    wf = jnp.concatenate(w, axis=0)
+    qf = jnp.concatenate(q, axis=0)
+    owner = lax.rem(lax.broadcasted_iota(jnp.int32, (tr, n), 0), rows)
+    for p in range(pairs):
+        for half in range(2):
+            mine = owner == 2 * p + half
+            wbd_ref[p, :, half * n : (half + 1) * n] = jnp.where(mine, wf, 0.0).astype(BF)
+            qbd_ref[p, :, half * n : (half + 1) * n] = jnp.where(mine, qf, 0.0).astype(BF)
+
+    hsel = lax.broadcasted_iota(jnp.int32, (heads, cols), 0)
+    hcol = lax.broadcasted_iota(jnp.int32, (heads, cols), 1) // HEAD_WIDTH
+
+    def spread(c, at):
+        expand = jnp.where(hsel == hcol + c * hb, 1.0, 0.0).astype(BF)
+        return dot(chi_ref[at], expand) + dot(clo_ref[at], expand)
+
+    def columns(c):
+        return pl.ds(pl.multiple_of(c * cols, cols), cols)
+
+    def inputs(c):
+        return [x_ref[t, :, columns(c)].astype(F32) for t in range(steps)]
+
+    def scaled_inputs(c):
+        e = spread(c, slice(0, tr))
+        x = inputs(c)
+        xe = jnp.concatenate([e[s * rows : (s + 1) * rows] * x[s] for s in range(steps)], axis=0)
+        xet_ref[lax.rem(c, 2)] = xe.T.astype(BF)
+
+    def gated_rows(c):
+        z = z_ref[lax.rem(c, 2)]
+        ce = spread(c, slice(tr, None))
+        x = inputs(c)
+        gain = gain_ref[:, columns(c)]
+        at = tr
+        out_rows = []
+        for t in range(steps):
+            y = ce[t * rows : (t + 1) * rows] * z[t * rows : (t + 1) * rows]
+            for s in range(t + 1):
+                y = y + ce[at : at + rows] * x[s]
+                at += rows
+            g = g_ref[t, :, columns(c)].astype(F32)
+            gated = y * (g / (1.0 + jnp.exp(-g)))
+            sq = gated * gated
+            part = sq[:, :LANES]
+            for b in range(1, cols // LANES):
+                part = part + sq[:, b * LANES : (b + 1) * LANES]
+            sq_ref[c, t * rows : (t + 1) * rows, :] = part
+            out_rows.append(gated * gain)
+        u_ref[:, columns(c)] = jnp.concatenate(out_rows, axis=0).astype(BF)
+
+    for i in (0, 1, 5, 8, 9):
+        copies[i].wait()
+    scaled_inputs(0)
+    z_ref[...] = jnp.zeros_like(z_ref)
+
+    def chunk(c, carry):
+        state_in(c).wait()
+        xet = xet_ref[lax.rem(c, 2)]
+        z = jnp.zeros((tr, cols), F32)
+        for p in range(pairs):
+            s0 = s_buf[2 * p, pl.ds(c * hb, hb)].reshape(cols, n)
+            s1 = s_buf[2 * p + 1, pl.ds(c * hb, hb)].reshape(cols, n)
+            z = z + dot(qbd_ref[p], jnp.concatenate([s0, s1], axis=1), NT)
+            up = dot(xet, wbd_ref[p])
+            for half, sv in ((0, s0), (1, s1)):
+                r = 2 * p + half
+                k4 = k4_ref[r, pl.ds(c * hb, hb), :]
+                grown = (
+                    k4[:, None, :] * sv.astype(F32).reshape(hb, HEAD_WIDTH, n)
+                    + up[:, half * n : (half + 1) * n].reshape(hb, HEAD_WIDTH, n)
+                )
+                o_buf[r, pl.ds(c * hb, hb)] = grown.astype(BF)
+        scaled_inputs(jnp.minimum(c + 1, chunks - 1))
+        gated_rows(jnp.maximum(c - 1, 0))
+        z_ref[lax.rem(c, 2)] = z
+        state_out(c).start()
+        return carry
+
+    lax.fori_loop(0, chunks, chunk, 0)
+    gated_rows(chunks - 1)
+    total = sq_ref[0]
+    for c in range(1, chunks):
+        total = total + sq_ref[c]
+    ss_ref[...] = total
+    which = lax.rem(lax.broadcasted_iota(jnp.int32, (tr, LANES), 0), rows)
+    slots = jnp.zeros((tr, LANES), F32)
+    for r in range(rows):
+        slots = jnp.where(which == r, store_buf[idx_buf[r]].astype(F32), slots)
+    u_ref[:, width:] = slots.astype(BF)
+    for c in range(chunks):
+        state_out(c).wait()
+
+
+def state_call(args, hb):
+    (idx, store, state, x, g, lg, w, q, rate, skip, gain) = args
+    steps, rows, width = x.shape
+    heads = rate.shape[1]
+    tr = steps * rows
+    n = w.shape[2]
+    cols = hb * HEAD_WIDTH
+    chunks = heads // hb
+    operands = [x, g, lg, rate, skip, gain, w, q, state, idx, store]
+    coef_rows = (steps * (steps + 1) // 2 + 2 * steps) * rows
+    scratch = [
+        pltpu.VMEM(x.shape, BF),
+        pltpu.VMEM(g.shape, BF),
+        pltpu.VMEM(lg.shape, F32),
+        pltpu.VMEM(rate.shape, F32),
+        pltpu.VMEM(skip.shape, F32),
+        pltpu.VMEM(gain.shape, F32),
+        pltpu.VMEM(w.shape, BF),
+        pltpu.VMEM(q.shape, BF),
+        pltpu.VMEM(state.shape, BF),
+        pltpu.VMEM(state.shape, BF),
+        pltpu.VMEM((coef_rows, heads), BF),
+        pltpu.VMEM((coef_rows, heads), BF),
+        pltpu.VMEM((rows // 2, tr, 2 * n), BF),
+        pltpu.VMEM((rows // 2, tr, 2 * n), BF),
+        pltpu.VMEM((rows, heads, LANES), F32),
+        pltpu.VMEM((2, cols, tr), BF),
+        pltpu.VMEM((2, tr, cols), F32),
+        pltpu.VMEM((chunks, tr, LANES), F32),
+        pltpu.SemaphoreType.DMA((10,)),
+        pltpu.SemaphoreType.DMA((chunks,)),
+        pltpu.SemaphoreType.DMA((chunks,)),
+        pltpu.SMEM(idx.shape, jnp.int32),
+        pltpu.SMEM(store.shape, jnp.int32),
+    ]
+    return pl.pallas_call(
+        functools.partial(state_body, hb),
+        in_specs=[ANY] * len(operands),
+        out_specs=[ANY, VM, VM],
+        out_shape=[
+            jax.ShapeDtypeStruct(state.shape, BF),
+            jax.ShapeDtypeStruct((tr, width + LANES), BF),
+            jax.ShapeDtypeStruct((tr, LANES), F32),
+        ],
+        scratch_shapes=scratch,
+        compiler_params=params(36),
+        cost_estimate=pl.CostEstimate(
+            flops=4 * tr * rows * heads * HEAD_WIDTH * n, bytes_accessed=4 * state.size, transcendentals=0
+        ),
+        name="state_steps",
+    )(*operands)
+
+
+def base_body(flips, features, u_ref, w_ref, *refs):
+    outs = refs[: len(flips)]
+    buf, acc, sems = refs[len(flips) :]
+    pieces = buf.shape[1]
+    depth = buf.shape[2]
+    me = lax.axis_index("tensor")
+
+    def fetch(k, i):
+        at = pl.multiple_of((me ^ flips[k]) * features, LANES)
+        return pltpu.make_async_copy(
+            w_ref.at[pl.ds(i * depth, depth), pl.ds(at, features)], buf.at[k, i], sems.at[k, i]
+        )
+
+    for k in range(len(flips)):
+        for i in range(pieces):
+            fetch(k, i).start()
+    for k in range(len(flips)):
+        for i in range(pieces):
+            fetch(k, i).wait()
+            tile = dot(u_ref[:, i * depth : (i + 1) * depth], buf[k, i])
+            if i == 0:
+                acc[...] = tile
+            elif i < pieces - 1:
+                acc[...] += tile
+            else:
+                outs[k][...] = (acc[...] + tile).astype(outs[k].dtype)
+
+
+def base_call(u, weight, flips, types, features, name):
+    tr = u.shape[0]
+    depth = weight.shape[0]
+    pieces = 4
+    count = len(flips)
+    return pl.pallas_call(
+        functools.partial(base_body, flips, features),
+        in_specs=[VM, ANY],
+        out_specs=[VM] * count,
+        out_shape=[jax.ShapeDtypeStruct((tr, features), t) for t in types],
+        scratch_shapes=[
+            pltpu.VMEM((count, pieces, depth // pieces, features), BF),
+            pltpu.VMEM((tr, features), F32),
+            pltpu.SemaphoreType.DMA((count, pieces)),
+        ],
+        compiler_params=params(20),
+        cost_estimate=pl.CostEstimate(
+            flops=2 * tr * depth * features * count,
+            bytes_accessed=2 * depth * features * count,
+            transcendentals=0,
+        ),
+        name=name,
+    )(u, weight)
+
+
+def down_body(sources, rank, *refs):
+    us = refs[:sources]
+    down_ref, ss_ref, out_ref, rows_ref = refs[sources:]
+    tr = us[0].shape[0]
+    wide, width = down_ref.shape
+    first = lax.axis_index("dp") * (wide // rank)
+    pad = jnp.zeros((LANES - tr, LANES), F32)
+    slots = []
+    for k in range(sources):
+        rows_ref[k, :tr] = us[k][:, :width]
+        rows_ref[k, tr:] = jnp.zeros((LANES - tr, width), BF)
+        column = jnp.concatenate([us[k][:, width:].astype(F32), pad - 1.0], axis=0)
+        slots.append(column.T[:1])
+    slots = jnp.concatenate(slots, axis=1)
+    lanes = sources * LANES
+    cell = lax.broadcasted_iota(jnp.int32, (wide, lanes), 0) // rank + first
+    part = dot(down_ref[...], rows_ref[...].reshape(lanes, width), NT)
+    part = jnp.where(cell.astype(F32) == slots, part, 0.0)
+    total = part[:rank]
+    for a in range(1, wide // rank):
+        total = total + part[a * rank : (a + 1) * rank]
+    ss = jnp.sum(jnp.concatenate([ss_ref[...], pad], axis=0).T, axis=0, keepdims=True)
+    hi = ss.astype(BF).astype(F32)
+    gap = jnp.zeros((1, lanes - LANES), F32)
+    row = lax.broadcasted_iota(jnp.int32, (EXT, lanes), 0)
+    tail = jnp.where(row == 0, slots, 0.0)
+    tail = jnp.where(row == 1, jnp.concatenate([hi, gap], axis=1), tail)
+    tail = jnp.where(row == 2, jnp.concatenate([ss - hi, gap], axis=1), tail)
+    out_ref[:rank] = total.astype(BF)
+    out_ref[rank:] = tail.astype(BF)
+
+
+def down_call(us, down, rank, ss):
+    sources = len(us)
+    tr = us[0].shape[0]
+    wide, width = down.shape
+    return pl.pallas_call(
+        functools.partial(down_body, sources, rank),
+        in_specs=[VM] * (sources + 2),
+        out_specs=VM,
+        out_shape=jax.ShapeDtypeStruct((rank + EXT, sources * LANES), BF),
+        scratch_shapes=[pltpu.VMEM((sources, LANES, width), BF)],
+        compiler_params=params(20),
+        cost_estimate=pl.CostEstimate(
+            flops=2 * sources * tr * wide * width, bytes_accessed=2 * wide * width, transcendentals=0
+        ),
+        name="adapter_down",
+    )(*us, down, ss)
+
+
+def up_body(rank, width, nmsg, *refs):
+    msgs = refs[:nmsg]
+    up_ref, here_ref, side_ref, far_ref, scale_ref, lhs_ref = refs[nmsg:]
+    tr = here_ref.shape[0]
+    wide = up_ref.shape[0]
+    sources = lhs_ref.shape[0]
+    total = msgs[0][:rank].astype(F32)
+    tail = msgs[0][rank:].astype(F32)
+    slots = tail[:1]
+    for m in msgs[1:]:
+        total = total + m[:rank].astype(F32)
+        tail = tail + m[rank:].astype(F32)
+    squares = tail[1:2, :LANES] + tail[2:3, :LANES]
+    scale = lax.rsqrt(squares / width + EPSILON)
+    scale = jnp.concatenate([scale, jnp.zeros((7, LANES), F32)], axis=0).T
+    scale_ref[...] = jnp.broadcast_to(scale[:tr, :1], (tr, LANES))
+    first = lax.axis_index("dp") * (wide // rank)
+    cell = (lax.broadcasted_iota(jnp.int32, (tr, wide), 1) // rank + first).astype(F32)
+    for k in range(sources):
+        mine = slice(k * LANES, (k + 1) * LANES)
+        twice = jnp.concatenate([total[:, mine], total[:, mine]], axis=0).T[:tr]
+        slot = jnp.broadcast_to(slots[:, mine], (8, LANES)).T[:tr, :1]
+        spread = jnp.concatenate([twice] * (wide // LANES), axis=1)
+        lhs_ref[k] = jnp.where(cell == slot, spread, 0.0).astype(BF)
+    delta = dot(lhs_ref[...].reshape(sources * tr, wide), up_ref[...])
+    here_ref[...] = delta[:tr].astype(BF)
+    side_ref[:tr] = delta[tr : 2 * tr].astype(BF)
+    far_ref[...] = delta[2 * tr : 3 * tr].astype(BF)
+    side_ref[tr:] = delta[3 * tr :].astype(BF)
+
+
+def up_call(msgs, up, rank, width, tr):
+    sources = msgs[0].shape[1] // LANES
+    wide, features = up.shape
+    return pl.pallas_call(
+        functools.partial(up_body, rank, width, len(msgs)),
+        in_specs=[VM] * (len(msgs) + 1),
+        out_specs=[VM] * 4,
+        out_shape=[
+            jax.ShapeDtypeStruct((tr, features), BF),
+            jax.ShapeDtypeStruct((2 * tr, features), BF),
+            jax.ShapeDtypeStruct((tr, features), BF),
+            jax.ShapeDtypeStruct((tr, LANES), F32),
+        ],
+        scratch_shapes=[pltpu.VMEM((sources, tr, wide), BF)],
+        compiler_params=params(16),
+        cost_estimate=pl.CostEstimate(
+            flops=2 * sources * tr * wide * features, bytes_accessed=2 * wide * features, transcendentals=0
+        ),
+        name="adapter_up",
+    )(*msgs, up)
+
+
+def swap(a, axis, size, bit):
+    return lax.ppermute(a, axis, [(i, i ^ bit) for i in range(size)])
+
+
+def after(a, *others):
+    return lax.optimization_barrier((a,) + others)[0]
+
+
+def per_device_pairs(
+    dp,
+    tensor,
+    row_adapter_index,
+    adapter_storage_row,
+    initial_head_state,
+    step_head_input,
+    step_gate_input,
+    step_size_logits,
+    state_write_key,
+    state_read_query,
+    head_decay_rate,
+    head_skip_gain,
+    gated_norm_gain,
+    output_weight,
+    adapter_down_weight,
+    adapter_up_weight,
+):
+    steps, rows, width = step_head_input.shape
+    tr = steps * rows
+    stored, _, rank = adapter_down_weight.shape
+    features = adapter_up_weight.shape[2]
+    down = jnp.swapaxes(adapter_down_weight, 1, 2).reshape(stored * rank, width)
+    up = adapter_up_weight.reshape(stored * rank, features)
+    weight = hbm(output_weight)
+    state_args = (
+        hbm(row_adapter_index),
+        hbm(adapter_storage_row),
+        hbm(initial_head_state),
+        hbm(step_head_input),
+        hbm(step_gate_input),
+        hbm(step_size_logits),
+        hbm(state_write_key),
+        hbm(state_read_query),
+        hbm(head_decay_rate[None]),
+        hbm(head_skip_gain[None]),
+        hbm(gated_norm_gain[None]),
+    )
+    carried, u, ss = state_call(state_args, 8)
+    far_u = swap(u, "dp", dp, 2)
+    near_u = swap(u, "dp", dp, 1)
+    (far,) = base_call(u, weight, (3,), [BF], features, "base_first")
+    near_in = swap(far, "tensor", tensor, 1)
+    mid, near, own = base_call(after(u, far), weight, (2, 1, 0), [F32, BF, F32], features, "base_rest")
+    both_u = swap(after(far_u, own), "dp", dp, 1)
+    near_own = swap(near, "tensor", tensor, 1)
+    mid = (mid + near_in.astype(F32)).astype(BF)
+    mid_in = swap(mid, "tensor", tensor, 2)
+    msg = down_call([after(u, mid), near_u, far_u, both_u], down, rank, ss)
+    msgs = [msg] + [swap(msg, "tensor", tensor, k) for k in range(1, tensor)]
+    here, side, over, scale = up_call(msgs, up, rank, width * tensor, tr)
+    side_in = swap(side, "dp", dp, 1)
+    over_in = swap(over + side_in[tr:], "dp", dp, 2)
+    total = own + near_own.astype(F32) + mid_in.astype(F32)
+    total = total + here.astype(F32) + side_in[:tr].astype(F32) + over_in.astype(F32)
+    mixed_out = (total * scale[:, :1]).astype(BF).reshape(steps, rows, features)
+    return mixed_out, carried
 
 
 def slot_lookup(row_adapter_index, adapter_storage_row):
@@ -17,7 +477,7 @@
     return jnp.sum(jnp.where(match, adapter_storage_row[None, :], 0), axis=1)
 
 
-def per_device(
+def per_device_any(
     row_adapter_index,
     adapter_storage_row,
     initial_head_state,
@@ -113,8 +573,12 @@
         P("dp", "tensor", None),
         P("dp", None, "tensor"),
     )
+    dp, tensor = mesh.shape["dp"], mesh.shape["tensor"]
+    body = per_device_any
+    if dp == 4 and tensor == 4:
+        body = functools.partial(per_device_pairs, dp, tensor)
     return jax.shard_map(
-        per_device,
+        body,
         mesh=mesh,
         in_specs=placed,
         out_specs=(P(None, ("groups", "dp"), "tensor"), P(("groups", "dp"), "tensor", None, None)),

time: 183 us -> 57.6 us (0.31)
  other arithmetic: 73.1 us -> 0.93 us
  blocking collectives: 44.1 us -> 0 us
  Pallas kernels: 0 us -> 24.1 us
  matrix products: 17.4 us -> 0 us
  between operations: 15.6 us -> 0.73 us
  starting transfers between devices: 0.13 us -> 14.3 us
  waiting for transfers between devices: 28.9 us -> 17.3 us
  local copies, waits for them, and re-layouts: 3.98 us -> 0.11 us
    reduce_sum x3 -> x0, other arithmetic: 62.5 us -> none  [the longest x1 62.2 us: per_device(): jnp.sum(updated * reader[:, None, None, :], axis=3)]
    psum x2 -> x0, blocking collectives: 38.8 us -> none  [the longest x1 25.3 us: per_device(): down_projected = lax.psum(picked, 'tensor').astype(jnp.bfloat16)]
    reduce_scatter x2 -> x0, waiting for transfers between devices: 26.7 us -> none  [the longest x1 26.7 us: per_device(): lax.psum_scatter(adapter_delta, 'dp', scatter_dimension=1, tiled=True)]
    pallas_call x0 -> x5, Pallas kernels: none -> 24.1 us  [the longest x1 12.8 us: state_call(): pl.pallas_call(functools.partial(state_body, hb), in_specs=[ANY] * len(op...]
    dot_general x3 -> x0, matrix products: 17.4 us -> none  [the longest x1 10.2 us: per_device(): jnp.dot(normed.reshape(steps_n * row_count, width), output_weight, prefer...]
    ppermute x0 -> x11, waiting for transfers between devices: none -> 17.3 us  [swap(): return lax.ppermute(a, axis, [(i, i ^ bit) for i in range(size)])]
    ppermute x0 -> x11, starting transfers between devices: none -> 14.3 us  [swap(): return lax.ppermute(a, axis, [(i, i ^ bit) for i in range(size)])]
    all_gather x1 -> x0, blocking collectives: 5.28 us -> none  [per_device(): lax.all_gather(marks, 'dp', axis=0, tiled=True)]
  transfers between devices with their start and end apart: 3 -> 11, of which waited for: 2 -> 6; matrix products, arithmetic and copies ran while one was open for 10% -> 0% of each run, Pallas kernels for 0% -> 14%
where the time goes in v2:
time: 57.6 us; the launch traced here: 57.5 us
  Pallas kernels  24.1 us (42%)
  waiting for transfers between devices  17.3 us (30%)
  starting transfers between devices  14.3 us (25%)
  other arithmetic  0.93 us (2%)
  between operations  0.73 us (1%)
    ppermute x11, waiting for transfers between devices, swap(): return lax.ppermute(a, axis, [(i, i ^ bit) for i in range(size)])  17.3 us
    ppermute x11, starting transfers between devices, swap(): return lax.ppermute(a, axis, [(i, i ^ bit) for i in range(size)])  14.3 us
    pallas_call x1, Pallas kernels, state_call(): pl.pallas_call(functools.partial(state_body, hb), in_specs=[ANY] * len(op...  12.8 us
    pallas_call x2, Pallas kernels, base_call(): pl.pallas_call(functools.partial(base_body, flips, features), in_specs=[V...  7.77 us
    pallas_call x1, Pallas kernels, down_call(): pl.pallas_call(functools.partial(down_body, sources, rank), in_specs=[VM]...  2.38 us
    pallas_call x1, Pallas kernels, up_call(): pl.pallas_call(functools.partial(up_body, rank, width, len(msgs)), in_spe...  1.18 us
  transfers between devices with their start and end apart: 11, of which 6 were waited for; matrix products, arithmetic and copies ran while one was open for 0% of the time, Pallas kernels for 14%

profile of v2, /device:TPU:0, one launch (start us, length us, event | category | flops | bytes accessed | tf_op | source)
XLA Modules:
  0.0 57.5 jit_solution(6460576806277808715)
XLA Ops:
  0.6 12.8 %state_steps.1 = (bf16[24,32,64,128]{3,2,1,0:T(8,128)(2,1)}, bf16[96,2176]{1,0:T(8,128)(2,1)S(1)}, f32[96,128]{1,0:T(8,128)S(1)}) custom-call(bf16[4,24,2048]{2,1,0:T(8,128)(2,1)} %refs_0_.1, bf16[4,24,2048]{2,1,0:T(8,128)(2,1)} %refs_1_.1, f32[4,24,32]{2,1,0:T(8,128)} %refs_2_.1, f32[1,32]{1,0:T(1,128)} %bitcast.12, f32[1,32]{1,0:T(1,128)} %bitcast.13, ...), custom_call_target="tpu_custom_call" | custom-call | flops 2415919104 | bytes 25165824 | tf_op jit(solution)/shard_map/state_steps/pallas_call | solution.py:232
  13.4 3.0 %collective-permute-start.4 = (bf16[96,2176]{1,0:T(8,128)(2,1)S(1)}, bf16[96,2176]{1,0:T(8,128)(2,1)S(1)}, u32[]{:S(2)}, u32[]{:S(2)}) collective-permute-start(bf16[96,2176]{1,0:T(8,128)(2,1)S(1)} %get-tuple-element.20.u_ref.refs_0_), channel_id=1, source_target_pairs={{0,8},{4,12},{8,0},{12,4},{1,9},{5,13},{9,1},{13,5},{2,10},{6,14},... | collective-permute-start | bytes 1253384 | tf_op jit(solution)/shard_map/ppermute | solution.py:407
  16.4 2.5 %base_first.1 = bf16[96,1024]{1,0:T(8,128)(2,1)S(1)} custom-call(bf16[96,2176]{1,0:T(8,128)(2,1)S(1)} %get-tuple-element.20.u_ref.refs_0_, bf16[2048,4096]{1,0:T(8,128)(2,1)} %w_ref.3), custom_call_target="tpu_custom_call" | custom-call | flops 402653184 | bytes 4194304 | tf_op jit(solution)/shard_map/base_first/pallas_call | solution.py:283
  19.0 0.0 copy-start.1
  19.0 1.6 %collective-permute-start.1 = (bf16[96,1024]{1,0:T(8,128)(2,1)S(1)}, bf16[96,1024]{1,0:T(8,128)(2,1)S(1)}, u32[]{:S(2)}, u32[]{:S(2)}) collective-permute-start(bf16[96,1024]{1,0:T(8,128)(2,1)S(1)} %base_first.1), channel_id=1, source_target_pairs={{0,1},{1,0},{2,3},{3,2},{4,5},{5,4},{6,7},{7,6},{8,9},{9,8},{10,11... | collective-permute-start | bytes 589832 | tf_op jit(solution)/shard_map/ppermute | solution.py:407
  20.6 5.2 %base_rest.1 = (f32[96,1024]{1,0:T(8,128)S(1)}, bf16[96,1024]{1,0:T(8,128)(2,1)S(1)}, f32[96,1024]{1,0:T(8,128)S(1)}) custom-call(bf16[96,2176]{1,0:T(8,128)(2,1)S(1)} %get-tuple-element.20.u_ref.refs_0_, bf16[2048,4096]{1,0:T(8,128)(2,1)} %w_ref.3), custom_call_target="tpu_custom_call" | custom-call | flops 1207959552 | bytes 12582912 | tf_op jit(solution)/shard_map/base_rest/pallas_call | solution.py:283
  25.9 0.2 collective-permute-done.4.refs_2_
  26.1 0.4 collective-permute-start.5
  26.5 1.3 %collective-permute-done.5.refs_3_ = bf16[96,2176]{1,0:T(8,128)(2,1)S(1)} collective-permute-done((bf16[96,2176]{1,0:T(8,128)(2,1)S(1)}, bf16[96,2176]{1,0:T(8,128)(2,1)S(1)}, u32[]{:S(2)}, u32[]{:S(2)}) %collective-permute-start.5) | collective-permute-done | bytes 417824 | tf_op jit(solution)/shard_map/ppermute | solution.py:407
  27.9 2.4 %adapter_down.1.refs_0_ = bf16[80,512]{1,0:T(8,128)(2,1)S(1)} custom-call(bf16[96,2176]{1,0:T(8,128)(2,1)S(1)} %get-tuple-element.20.u_ref.refs_0_, bf16[96,2176]{1,0:T(8,128)(2,1)S(1)} %collective-permute-done.3.refs_1_, bf16[96,2176]{1,0:T(8,128)(2,1)S(1)} %collective-permute-done.4.refs_2_, bf16[96,2176]{1,0:T(8,128)(2,1)S(1)} %collective-permute-done.5.refs_3_, ...), custom_call_target="tpu_custom_call" | custom-call | flops 1610612736 | bytes 4194304 | tf_op jit(solution)/shard_map/adapter_down/pallas_call | solution.py:339
  30.2 1.9 %collective-permute-start.6 = (bf16[80,512]{1,0:T(8,128)(2,1)S(1)}, bf16[80,512]{1,0:T(8,128)(2,1)S(1)}, u32[]{:S(2)}, u32[]{:S(2)}) collective-permute-start(bf16[80,512]{1,0:T(8,128)(2,1)S(1)} %adapter_down.1.refs_0_), channel_id=1, source_target_pairs={{0,1},{1,0},{2,3},{3,2},{4,5},{5,4},{6,7},{7,6},{8,9},{9,8},{10,11... | collective-permute-start | bytes 245768 | tf_op jit(solution)/shard_map/ppermute | solution.py:407
  32.1 2.6 %collective-permute-start.7 = (bf16[80,512]{1,0:T(8,128)(2,1)S(1)}, bf16[80,512]{1,0:T(8,128)(2,1)S(1)}, u32[]{:S(2)}, u32[]{:S(2)}) collective-permute-start(bf16[80,512]{1,0:T(8,128)(2,1)S(1)} %adapter_down.1.refs_0_), channel_id=1, source_target_pairs={{0,2},{1,3},{2,0},{3,1},{4,6},{5,7},{6,4},{7,5},{8,10},{9,11},{10,... | collective-permute-start | bytes 245768 | tf_op jit(solution)/shard_map/ppermute | solution.py:407
  34.7 0.0 collective-permute-start.8
  34.7 0.3 collective-permute-done.6.refs_1_
  35.0 6.5 %collective-permute-done.7.refs_2_ = bf16[80,512]{1,0:T(8,128)(2,1)S(1)} collective-permute-done((bf16[80,512]{1,0:T(8,128)(2,1)S(1)}, bf16[80,512]{1,0:T(8,128)(2,1)S(1)}, u32[]{:S(2)}, u32[]{:S(2)}) %collective-permute-start.7) | collective-permute-done | bytes 81952 | tf_op jit(solution)/shard_map/ppermute | solution.py:407
  41.6 1.2 %adapter_up.1 = (bf16[96,1024]{1,0:T(8,128)(2,1)S(1)}, bf16[192,1024]{1,0:T(8,128)(2,1)S(1)}, bf16[96,1024]{1,0:T(8,128)(2,1)S(1)}, f32[96,128]{1,0:T(8,128)S(1)}) custom-call(bf16[80,512]{1,0:T(8,128)(2,1)S(1)} %adapter_down.1.refs_0_, bf16[80,512]{1,0:T(8,128)(2,1)S(1)} %collective-permute-done.6.refs_1_, ...), custom_call_target="tpu_custom_call" | custom-call | flops 805306368 | bytes 2097152 | tf_op jit(solution)/shard_map/adapter_up/pallas_call | solution.py:387
  42.8 0.1 collective-permute-start.9
  42.8 1.6 %collective-permute-start = (bf16[96,1024]{1,0:T(8,128)(2,1)S(1)}, bf16[96,1024]{1,0:T(8,128)(2,1)S(1)}, u32[]{:S(2)}, u32[]{:S(2)}) collective-permute-start(bf16[96,1024]{1,0:T(8,128)(2,1)S(1)} %get-tuple-element.18), channel_id=1, source_target_pairs={{0,1},{1,0},{2,3},{3,2},{4,5},{5,4},{6,7},{7,6},{8,9},{9,8},{10,11... | collective-permute-start | bytes 589832 | tf_op jit(solution)/shard_map/ppermute | solution.py:407
  44.5 1.5 %collective-permute-start.2 = (bf16[96,1024]{1,0:T(8,128)(2,1)S(1)}, bf16[96,1024]{1,0:T(8,128)(2,1)S(1)}, u32[]{:S(2)}, u32[]{:S(2)}) collective-permute-start(bf16[96,1024]{1,0:T(8,128)(2,1)S(1)} %add_convert_fusion), channel_id=1, source_target_pairs={{0,2},{1,3},{2,0},{3,1},{4,6},{5,7},{6,4},{7,5},{8,10},{9,11},{10,... | collective-permute-start | bytes 589832 | tf_op jit(solution)/shard_map/ppermute | solution.py:407
  46.0 1.5 %collective-permute-start.10 = (bf16[96,1024]{1,0:T(8,128)(2,1)S(1)}, bf16[96,1024]{1,0:T(8,128)(2,1)S(1)}, u32[]{:S(2)}, u32[]{:S(2)}) collective-permute-start(bf16[96,1024]{1,0:T(8,128)(2,1)S(1)} %slice_add_fusion), channel_id=1, source_target_pairs={{0,8},{4,12},{8,0},{12,4},{1,9},{5,13},{9,1},{13,5},{2,10},{6,14},... | collective-permute-start | bytes 589832 | tf_op jit(solution)/shard_map/ppermute | solution.py:407
  47.6 0.1 slice_reduce_fusion
  47.7 6.5 %collective-permute-done = bf16[96,1024]{1,0:T(8,128)(2,1)S(1)} collective-permute-done((bf16[96,1024]{1,0:T(8,128)(2,1)S(1)}, bf16[96,1024]{1,0:T(8,128)(2,1)S(1)}, u32[]{:S(2)}, u32[]{:S(2)}) %collective-permute-start) | collective-permute-done | bytes 196640 | tf_op jit(solution)/shard_map/ppermute | solution.py:407
  54.2 2.4 %collective-permute-done.2 = bf16[96,1024]{1,0:T(8,128)(2,1)S(1)} collective-permute-done((bf16[96,1024]{1,0:T(8,128)(2,1)S(1)}, bf16[96,1024]{1,0:T(8,128)(2,1)S(1)}, u32[]{:S(2)}, u32[]{:S(2)}) %collective-permute-start.2) | collective-permute-done | bytes 196640 | tf_op jit(solution)/shard_map/ppermute | solution.py:407
  56.6 0.9 %multiply_convert_fusion = bf16[96,1024]{1,0:T(8,128)(2,1)} fusion(bf16[96,1024]{1,0:T(8,128)(2,1)S(1)} %collective-permute-done.10, bf16[96,1024]{1,0:T(8,128)(2,1)S(1)} %get-tuple-element.23, bf16[96,1024]{1,0:T(8,128)(2,1)S(1)} %collective-permute-done.2, f32[96,1024]{1,0:T(8,128)S(1)} %get-tuple-element.17, bf16[96,1024]{1,0:T(8,128)(2,1)S(1)} %collective-permute-done, ...), kind=kLoop, calls=%fused_computation | loop fusion | flops 1179648 | bytes 1573248 | tf_op jit(solution)/shard_map/convert_element_type | solution.py:469
  (11 shorter events, 0.1 us)
Async XLA Ops:
  13.4 12.6 %collective-permute-start.4 = (bf16[96,2176]{1,0:T(8,128)(2,1)S(1)}, bf16[96,2176]{1,0:T(8,128)(2,1)S(1)}, u32[]{:S(2)}, u32[]{:S(2)}) collective-permute-start(bf16[96,2176]{1,0:T(8,128)(2,1)S(1)} %get-tuple-element.20.u_ref.refs_0_), channel_id=1, source_target_pairs={{0,8},{4,12},{8,0},{12,4},{1,9},{5,13},{9,1},{13,5},{2,10},{6,14},... | collective-permute-start | bytes 1253384 | tf_op jit(solution)/shard_map/ppermute | solution.py:407
  16.4 10.1 %collective-permute-start.3 = (bf16[96,2176]{1,0:T(8,128)(2,1)S(1)}, bf16[96,2176]{1,0:T(8,128)(2,1)S(1)}, u32[]{:S(2)}, u32[]{:S(2)}) collective-permute-start(bf16[96,2176]{1,0:T(8,128)(2,1)S(1)} %get-tuple-element.20.u_ref.refs_0_), channel_id=1, source_target_pairs={{0,4},{4,0},{8,12},{12,8},{1,5},{5,1},{9,13},{13,9},{2,6},{6,2},{1... | collective-permute-start | bytes 1253384 | tf_op jit(solution)/shard_map/ppermute | solution.py:407
  19.0 8.9 %copy-start = (bf16[16,2048,64]{1,2,0:T(8,128)(2,1)S(1)}, bf16[16,2048,64]{1,2,0:T(8,128)(2,1)}, u32[]{:S(2)}) copy-start(bf16[16,2048,64]{1,2,0:T(8,128)(2,1)} %param.26) | copy-start | bytes 12582916
  19.0 22.6 %copy-start.1 = (bf16[16,64,1024]{2,1,0:T(8,128)(2,1)S(1)}, bf16[16,64,1024]{2,1,0:T(8,128)(2,1)}, u32[]{:S(2)}) copy-start(bf16[16,64,1024]{2,1,0:T(8,128)(2,1)} %param.27) | copy-start | bytes 6291460
  19.0 7.5 %collective-permute-start.1 = (bf16[96,1024]{1,0:T(8,128)(2,1)S(1)}, bf16[96,1024]{1,0:T(8,128)(2,1)S(1)}, u32[]{:S(2)}, u32[]{:S(2)}) collective-permute-start(bf16[96,1024]{1,0:T(8,128)(2,1)S(1)} %base_first.1), channel_id=1, source_target_pairs={{0,1},{1,0},{2,3},{3,2},{4,5},{5,4},{6,7},{7,6},{8,9},{9,8},{10,11... | collective-permute-start | bytes 589832 | tf_op jit(solution)/shard_map/ppermute | solution.py:407
  26.1 1.8 %collective-permute-start.5 = (bf16[96,2176]{1,0:T(8,128)(2,1)S(1)}, bf16[96,2176]{1,0:T(8,128)(2,1)S(1)}, u32[]{:S(2)}, u32[]{:S(2)}) collective-permute-start(bf16[96,2176]{1,0:T(8,128)(2,1)S(1)} %collective-permute-done.4.refs_2_), channel_id=1, source_target_pairs={{0,4},{4,0},{8,12},{12,8},{1,5},{5,1},{9,13},{13,9},{2,6},{6,2},{1... | collective-permute-start | bytes 1253384 | tf_op jit(solution)/shard_map/ppermute | solution.py:407
  30.2 4.8 %collective-permute-start.6 = (bf16[80,512]{1,0:T(8,128)(2,1)S(1)}, bf16[80,512]{1,0:T(8,128)(2,1)S(1)}, u32[]{:S(2)}, u32[]{:S(2)}) collective-permute-start(bf16[80,512]{1,0:T(8,128)(2,1)S(1)} %adapter_down.1.refs_0_), channel_id=1, source_target_pairs={{0,1},{1,0},{2,3},{3,2},{4,5},{5,4},{6,7},{7,6},{8,9},{9,8},{10,11... | collective-permute-start | bytes 245768 | tf_op jit(solution)/shard_map/ppermute | solution.py:407
  32.1 9.5 %collective-permute-start.7 = (bf16[80,512]{1,0:T(8,128)(2,1)S(1)}, bf16[80,512]{1,0:T(8,128)(2,1)S(1)}, u32[]{:S(2)}, u32[]{:S(2)}) collective-permute-start(bf16[80,512]{1,0:T(8,128)(2,1)S(1)} %adapter_down.1.refs_0_), channel_id=1, source_target_pairs={{0,2},{1,3},{2,0},{3,1},{4,6},{5,7},{6,4},{7,5},{8,10},{9,11},{10,... | collective-permute-start | bytes 245768 | tf_op jit(solution)/shard_map/ppermute | solution.py:407
  34.7 6.9 %collective-permute-start.8 = (bf16[80,512]{1,0:T(8,128)(2,1)S(1)}, bf16[80,512]{1,0:T(8,128)(2,1)S(1)}, u32[]{:S(2)}, u32[]{:S(2)}) collective-permute-start(bf16[80,512]{1,0:T(8,128)(2,1)S(1)} %adapter_down.1.refs_0_), channel_id=1, source_target_pairs={{0,3},{1,2},{2,1},{3,0},{4,7},{5,6},{6,5},{7,4},{8,11},{9,10},{10,... | collective-permute-start | bytes 245768 | tf_op jit(solution)/shard_map/ppermute | solution.py:407
  42.8 3.2 %collective-permute-start.9 = (bf16[192,1024]{1,0:T(8,128)(2,1)S(1)}, bf16[192,1024]{1,0:T(8,128)(2,1)S(1)}, u32[]{:S(2)}, u32[]{:S(2)}) collective-permute-start(bf16[192,1024]{1,0:T(8,128)(2,1)S(1)} %get-tuple-element.24), channel_id=1, source_target_pairs={{0,4},{4,0},{8,12},{12,8},{1,5},{5,1},{9,13},{13,9},{2,6},{6,2},{1... | collective-permute-start | bytes 1179656 | tf_op jit(solution)/shard_map/ppermute | solution.py:407
  42.8 11.3 %collective-permute-start = (bf16[96,1024]{1,0:T(8,128)(2,1)S(1)}, bf16[96,1024]{1,0:T(8,128)(2,1)S(1)}, u32[]{:S(2)}, u32[]{:S(2)}) collective-permute-start(bf16[96,1024]{1,0:T(8,128)(2,1)S(1)} %get-tuple-element.18), channel_id=1, source_target_pairs={{0,1},{1,0},{2,3},{3,2},{4,5},{5,4},{6,7},{7,6},{8,9},{9,8},{10,11... | collective-permute-start | bytes 589832 | tf_op jit(solution)/shard_map/ppermute | solution.py:407
  44.5 12.1 %collective-permute-start.2 = (bf16[96,1024]{1,0:T(8,128)(2,1)S(1)}, bf16[96,1024]{1,0:T(8,128)(2,1)S(1)}, u32[]{:S(2)}, u32[]{:S(2)}) collective-permute-start(bf16[96,1024]{1,0:T(8,128)(2,1)S(1)} %add_convert_fusion), channel_id=1, source_target_pairs={{0,2},{1,3},{2,0},{3,1},{4,6},{5,7},{6,4},{7,5},{8,10},{9,11},{10,... | collective-permute-start | bytes 589832 | tf_op jit(solution)/shard_map/ppermute | solution.py:407
  46.0 10.6 %collective-permute-start.10 = (bf16[96,1024]{1,0:T(8,128)(2,1)S(1)}, bf16[96,1024]{1,0:T(8,128)(2,1)S(1)}, u32[]{:S(2)}, u32[]{:S(2)}) collective-permute-start(bf16[96,1024]{1,0:T(8,128)(2,1)S(1)} %slice_add_fusion), channel_id=1, source_target_pairs={{0,8},{4,12},{8,0},{12,4},{1,9},{5,13},{9,1},{13,5},{2,10},{6,14},... | collective-permute-start | bytes 589832 | tf_op jit(solution)/shard_map/ppermute | solution.py:407

commit v3 on v2

--- a/solution.py
+++ b/solution.py
@@ -305,29 +305,27 @@
     down_ref, ss_ref, out_ref, rows_ref = refs[sources:]
     tr = us[0].shape[0]
     wide, width = down_ref.shape
+    lanes = sources * tr
     first = lax.axis_index("dp") * (wide // rank)
-    pad = jnp.zeros((LANES - tr, LANES), F32)
     slots = []
     for k in range(sources):
-        rows_ref[k, :tr] = us[k][:, :width]
-        rows_ref[k, tr:] = jnp.zeros((LANES - tr, width), BF)
-        column = jnp.concatenate([us[k][:, width:].astype(F32), pad - 1.0], axis=0)
-        slots.append(column.T[:1])
-    slots = jnp.concatenate(slots, axis=1)
-    lanes = sources * LANES
+        rows_ref[k * tr : (k + 1) * tr] = us[k][:, :width]
+        slots.append(us[k][:, width:].astype(F32))
+    slots = jnp.concatenate(slots, axis=0).T[:1]
     cell = lax.broadcasted_iota(jnp.int32, (wide, lanes), 0) // rank + first
-    part = dot(down_ref[...], rows_ref[...].reshape(lanes, width), NT)
+    part = dot(down_ref[...], rows_ref[...], NT)
     part = jnp.where(cell.astype(F32) == slots, part, 0.0)
     total = part[:rank]
     for a in range(1, wide // rank):
         total = total + part[a * rank : (a + 1) * rank]
-    ss = jnp.sum(jnp.concatenate([ss_ref[...], pad], axis=0).T, axis=0, keepdims=True)
+    ss = jnp.sum(ss_ref[...].T, axis=0, keepdims=True)
     hi = ss.astype(BF).astype(F32)
-    gap = jnp.zeros((1, lanes - LANES), F32)
+    gap = jnp.zeros((1, lanes - tr), F32)
     row = lax.broadcasted_iota(jnp.int32, (EXT, lanes), 0)
+    at = 1 + 2 * lax.rem(lax.axis_index("tensor"), 2)
     tail = jnp.where(row == 0, slots, 0.0)
-    tail = jnp.where(row == 1, jnp.concatenate([hi, gap], axis=1), tail)
-    tail = jnp.where(row == 2, jnp.concatenate([ss - hi, gap], axis=1), tail)
+    tail = jnp.where(row == at, jnp.concatenate([hi, gap], axis=1), tail)
+    tail = jnp.where(row == at + 1, jnp.concatenate([ss - hi, gap], axis=1), tail)
     out_ref[:rank] = total.astype(BF)
     out_ref[rank:] = tail.astype(BF)
 
@@ -340,8 +338,8 @@
         functools.partial(down_body, sources, rank),
         in_specs=[VM] * (sources + 2),
         out_specs=VM,
-        out_shape=jax.ShapeDtypeStruct((rank + EXT, sources * LANES), BF),
-        scratch_shapes=[pltpu.VMEM((sources, LANES, width), BF)],
+        out_shape=jax.ShapeDtypeStruct((rank + EXT, sources * tr), BF),
+        scratch_shapes=[pltpu.VMEM((sources * tr, width), BF)],
         compiler_params=params(20),
         cost_estimate=pl.CostEstimate(
             flops=2 * sources * tr * wide * width, bytes_accessed=2 * wide * width, transcendentals=0
@@ -350,57 +348,67 @@
     )(*us, down, ss)
 
 
-def up_body(rank, width, nmsg, *refs):
-    msgs = refs[:nmsg]
-    up_ref, here_ref, side_ref, far_ref, scale_ref, lhs_ref = refs[nmsg:]
+def up_body(rank, width, own_ref, pair_ref, other_ref, up_ref, here_ref, near_ref, far_ref, both_ref, scale_ref):
     tr = here_ref.shape[0]
     wide = up_ref.shape[0]
-    sources = lhs_ref.shape[0]
-    total = msgs[0][:rank].astype(F32)
-    tail = msgs[0][rank:].astype(F32)
-    slots = tail[:1]
-    for m in msgs[1:]:
-        total = total + m[:rank].astype(F32)
-        tail = tail + m[rank:].astype(F32)
-    squares = tail[1:2, :LANES] + tail[2:3, :LANES]
-    scale = lax.rsqrt(squares / width + EPSILON)
-    scale = jnp.concatenate([scale, jnp.zeros((7, LANES), F32)], axis=0).T
+    lanes = own_ref.shape[1]
+    slots = own_ref[rank:].astype(F32)[:1]
+    total = pair_ref[:rank].astype(F32) + other_ref[:rank].astype(F32)
+    tail = pair_ref[rank:].astype(F32) + other_ref[rank:].astype(F32)
+    tail = tail[:, :LANES]
+    squares = (tail[1:2] + tail[2:3]) + (tail[3:4] + tail[4:5])
+    scale = jnp.broadcast_to(lax.rsqrt(squares / width + EPSILON), (8, LANES)).T
     scale_ref[...] = jnp.broadcast_to(scale[:tr, :1], (tr, LANES))
     first = lax.axis_index("dp") * (wide // rank)
-    cell = (lax.broadcasted_iota(jnp.int32, (tr, wide), 1) // rank + first).astype(F32)
-    for k in range(sources):
-        mine = slice(k * LANES, (k + 1) * LANES)
-        twice = jnp.concatenate([total[:, mine], total[:, mine]], axis=0).T[:tr]
-        slot = jnp.broadcast_to(slots[:, mine], (8, LANES)).T[:tr, :1]
-        spread = jnp.concatenate([twice] * (wide // LANES), axis=1)
-        lhs_ref[k] = jnp.where(cell == slot, spread, 0.0).astype(BF)
-    delta = dot(lhs_ref[...].reshape(sources * tr, wide), up_ref[...])
+    cell = (lax.broadcasted_iota(jnp.int32, (lanes, wide), 1) // rank + first).astype(F32)
+    twice = jnp.concatenate([total] * (LANES // rank), axis=0).T.astype(BF).astype(F32)
+    slot = jnp.broadcast_to(slots, (8, lanes)).T[:, :1]
+    spread = jnp.concatenate([twice] * (wide // LANES), axis=1)
+    rows = jnp.where(cell == slot, spread, 0.0).astype(BF)
+    delta = dot(rows, up_ref[...])
     here_ref[...] = delta[:tr].astype(BF)
-    side_ref[:tr] = delta[tr : 2 * tr].astype(BF)
+    near_ref[...] = delta[tr : 2 * tr].astype(BF)
     far_ref[...] = delta[2 * tr : 3 * tr].astype(BF)
-    side_ref[tr:] = delta[3 * tr :].astype(BF)
-
-
-def up_call(msgs, up, rank, width, tr):
-    sources = msgs[0].shape[1] // LANES
+    both_ref[...] = delta[3 * tr :].astype(BF)
+
+
+def up_call(own, pair, other, up, rank, width, tr):
+    lanes = own.shape[1]
     wide, features = up.shape
     return pl.pallas_call(
-        functools.partial(up_body, rank, width, len(msgs)),
-        in_specs=[VM] * (len(msgs) + 1),
-        out_specs=[VM] * 4,
+        functools.partial(up_body, rank, width),
+        in_specs=[VM] * 4,
+        out_specs=[VM] * 5,
         out_shape=[
             jax.ShapeDtypeStruct((tr, features), BF),
-            jax.ShapeDtypeStruct((2 * tr, features), BF),
+            jax.ShapeDtypeStruct((tr, features), BF),
+            jax.ShapeDtypeStruct((tr, features), BF),
             jax.ShapeDtypeStruct((tr, features), BF),
             jax.ShapeDtypeStruct((tr, LANES), F32),
         ],
-        scratch_shapes=[pltpu.VMEM((sources, tr, wide), BF)],
         compiler_params=params(16),
         cost_estimate=pl.CostEstimate(
-            flops=2 * sources * tr * wide * features, bytes_accessed=2 * wide * features, transcendentals=0
+            flops=2 * lanes * wide * features, bytes_accessed=2 * wide * features, transcendentals=0
         ),
         name="adapter_up",
-    )(*msgs, up)
+    )(own, pair, other, up)
+
+
+def sum_body(own_ref, mid_ref, here_ref, side_ref, out_ref):
+    total = own_ref[...] + mid_ref[...].astype(F32)
+    out_ref[...] = total + here_ref[...].astype(F32) + side_ref[...].astype(F32)
+
+
+def sum_call(own, mid, here, side):
+    return pl.pallas_call(
+        sum_body,
+        in_specs=[VM] * 4,
+        out_specs=VM,
+        out_shape=jax.ShapeDtypeStruct(own.shape, F32),
+        compiler_params=params(8),
+        cost_estimate=pl.CostEstimate(flops=4 * own.size, bytes_accessed=2000000, transcendentals=0),
+        name="sum_parts",
+    )(own, mid, here, side)
 
 
 def swap(a, axis, size, bit):
@@ -460,13 +468,14 @@
     mid = (mid + near_in.astype(F32)).astype(BF)
     mid_in = swap(mid, "tensor", tensor, 2)
     msg = down_call([after(u, mid), near_u, far_u, both_u], down, rank, ss)
-    msgs = [msg] + [swap(msg, "tensor", tensor, k) for k in range(1, tensor)]
-    here, side, over, scale = up_call(msgs, up, rank, width * tensor, tr)
+    pair = (msg.astype(F32) + swap(msg, "tensor", tensor, 1).astype(F32)).astype(BF)
+    other = swap(pair, "tensor", tensor, 2)
+    here, side, over, both, scale = up_call(after(msg, near_own), pair, other, up, rank, width * tensor, tr)
+    both_in = swap(both, "dp", dp, 1)
     side_in = swap(side, "dp", dp, 1)
-    over_in = swap(over + side_in[tr:], "dp", dp, 2)
-    total = own + near_own.astype(F32) + mid_in.astype(F32)
-    total = total + here.astype(F32) + side_in[:tr].astype(F32) + over_in.astype(F32)
-    mixed_out = (total * scale[:, :1]).astype(BF).reshape(steps, rows, features)
+    over_in = swap(over + both_in, "dp", dp, 2)
+    half = sum_call(own, mid_in, here, side_in)
+    mixed_out = ((half + near_own.astype(F32) + over_in.astype(F32)) * scale[:, :1]).astype(BF).reshape(steps, rows, features)
     return mixed_out, carried
 
 

time: 57.6 us -> 55 us (0.955)
  waiting for transfers between devices: 17.3 us -> 14.1 us
    ppermute x11, waiting for transfers between devices: 17.3 us -> 14.1 us  [swap(): return lax.ppermute(a, axis, [(i, i ^ bit) for i in range(size)])]
    pallas_call x1 -> x2, Pallas kernels: 1.18 us -> 1.35 us  [the longest x1 1.25 us: up_call(): pl.pallas_call(functools.partial(up_body, rank, width), in_specs=[VM] * 4...]
  transfers between devices with their start and end apart: 11 -> 11, of which waited for: 6 -> 5; matrix products, arithmetic and copies ran while one was open for 0% -> 0% of each run, Pallas kernels for 14% -> 14%
where the time goes in v3:
time: 55 us; the launch traced here: 54.8 us
  Pallas kernels  24.3 us (44%)
  starting transfers between devices  14.7 us (27%)
  waiting for transfers between devices  14.1 us (26%)
  other arithmetic  0.88 us (2%)
  between operations  0.75 us (1%)
    ppermute x11, starting transfers between devices, swap(): return lax.ppermute(a, axis, [(i, i ^ bit) for i in range(size)])  14.7 us
    ppermute x11, waiting for transfers between devices, swap(): return lax.ppermute(a, axis, [(i, i ^ bit) for i in range(size)])  14.1 us
    pallas_call x1, Pallas kernels, state_call(): pl.pallas_call(functools.partial(state_body, hb), in_specs=[ANY] * len(op...  12.8 us
    pallas_call x2, Pallas kernels, base_call(): pl.pallas_call(functools.partial(base_body, flips, features), in_specs=[V...  7.77 us
    pallas_call x1, Pallas kernels, down_call(): pl.pallas_call(functools.partial(down_body, sources, rank), in_specs=[VM]...  2.35 us
    pallas_call x1, Pallas kernels, up_call(): pl.pallas_call(functools.partial(up_body, rank, width), in_specs=[VM] * 4...  1.25 us
  transfers between devices with their start and end apart: 11, of which 5 were waited for; matrix products, arithmetic and copies ran while one was open for 0% of the time, Pallas kernels for 14%

profile of v3, /device:TPU:0, one launch (start us, length us, event | category | flops | bytes accessed | tf_op | source)
XLA Modules:
  0.0 54.8 jit_solution(6179653937280790033)
XLA Ops:
  0.6 12.8 %state_steps.1 = (bf16[24,32,64,128]{3,2,1,0:T(8,128)(2,1)}, bf16[96,2176]{1,0:T(8,128)(2,1)S(1)}, f32[96,128]{1,0:T(8,128)S(1)}) custom-call(bf16[4,24,2048]{2,1,0:T(8,128)(2,1)} %refs_0_.1, bf16[4,24,2048]{2,1,0:T(8,128)(2,1)} %refs_1_.1, f32[4,24,32]{2,1,0:T(8,128)} %refs_2_.1, f32[1,32]{1,0:T(1,128)} %bitcast.12, f32[1,32]{1,0:T(1,128)} %bitcast.13, ...), custom_call_target="tpu_custom_call" | custom-call | flops 2415919104 | bytes 25165824 | tf_op jit(solution)/shard_map/state_steps/pallas_call | solution.py:232
  13.4 3.0 %collective-permute-start.3 = (bf16[96,2176]{1,0:T(8,128)(2,1)S(1)}, bf16[96,2176]{1,0:T(8,128)(2,1)S(1)}, u32[]{:S(2)}, u32[]{:S(2)}) collective-permute-start(bf16[96,2176]{1,0:T(8,128)(2,1)S(1)} %get-tuple-element.21.u_ref.refs_0_), channel_id=1, source_target_pairs={{0,8},{4,12},{8,0},{12,4},{1,9},{5,13},{9,1},{13,5},{2,10},{6,14},... | collective-permute-start | bytes 1253384 | tf_op jit(solution)/shard_map/ppermute | solution.py:415
  16.4 2.5 %base_first.1 = bf16[96,1024]{1,0:T(8,128)(2,1)S(1)} custom-call(bf16[96,2176]{1,0:T(8,128)(2,1)S(1)} %get-tuple-element.21.u_ref.refs_0_, bf16[2048,4096]{1,0:T(8,128)(2,1)} %w_ref.3), custom_call_target="tpu_custom_call" | custom-call | flops 402653184 | bytes 4194304 | tf_op jit(solution)/shard_map/base_first/pallas_call | solution.py:283
  19.0 0.0 copy-start
  19.0 1.6 %collective-permute-start = (bf16[96,1024]{1,0:T(8,128)(2,1)S(1)}, bf16[96,1024]{1,0:T(8,128)(2,1)S(1)}, u32[]{:S(2)}, u32[]{:S(2)}) collective-permute-start(bf16[96,1024]{1,0:T(8,128)(2,1)S(1)} %base_first.1), channel_id=1, source_target_pairs={{0,1},{1,0},{2,3},{3,2},{4,5},{5,4},{6,7},{7,6},{8,9},{9,8},{10,11... | collective-permute-start | bytes 589832 | tf_op jit(solution)/shard_map/ppermute | solution.py:415
  20.6 5.2 %base_rest.1 = (f32[96,1024]{1,0:T(8,128)S(1)}, bf16[96,1024]{1,0:T(8,128)(2,1)S(1)}, f32[96,1024]{1,0:T(8,128)S(1)}) custom-call(bf16[96,2176]{1,0:T(8,128)(2,1)S(1)} %get-tuple-element.21.u_ref.refs_0_, bf16[2048,4096]{1,0:T(8,128)(2,1)} %w_ref.3), custom_call_target="tpu_custom_call" | custom-call | flops 1207959552 | bytes 12582912 | tf_op jit(solution)/shard_map/base_rest/pallas_call | solution.py:283
  25.9 0.2 collective-permute-done.3.refs_2_
  26.1 0.4 collective-permute-start.4
  26.5 1.3 %collective-permute-done.4.refs_3_ = bf16[96,2176]{1,0:T(8,128)(2,1)S(1)} collective-permute-done((bf16[96,2176]{1,0:T(8,128)(2,1)S(1)}, bf16[96,2176]{1,0:T(8,128)(2,1)S(1)}, u32[]{:S(2)}, u32[]{:S(2)}) %collective-permute-start.4) | collective-permute-done | bytes 417824 | tf_op jit(solution)/shard_map/ppermute | solution.py:415
  27.9 2.4 %adapter_down.1.own_ref = bf16[80,384]{1,0:T(8,128)(2,1)S(1)} custom-call(bf16[96,2176]{1,0:T(8,128)(2,1)S(1)} %get-tuple-element.21.u_ref.refs_0_, bf16[96,2176]{1,0:T(8,128)(2,1)S(1)} %collective-permute-done.2.refs_1_, bf16[96,2176]{1,0:T(8,128)(2,1)S(1)} %collective-permute-done.3.refs_2_, bf16[96,2176]{1,0:T(8,128)(2,1)S(1)} %collective-permute-done.4.refs_3_, ...), custom_call_target="tpu_custom_call" | custom-call | flops 1610612736 | bytes 4194304 | tf_op jit(solution)/shard_map/adapter_down/pallas_call | solution.py:337
  30.2 1.9 %collective-permute-start.6 = (bf16[80,384]{1,0:T(8,128)(2,1)S(1)}, bf16[80,384]{1,0:T(8,128)(2,1)S(1)}, u32[]{:S(2)}, u32[]{:S(2)}) collective-permute-start(bf16[80,384]{1,0:T(8,128)(2,1)S(1)} %adapter_down.1.own_ref), channel_id=1, source_target_pairs={{0,1},{1,0},{2,3},{3,2},{4,5},{5,4},{6,7},{7,6},{8,9},{9,8},{10,11... | collective-permute-start | bytes 184328 | tf_op jit(solution)/shard_map/ppermute | solution.py:415
  32.1 0.2 collective-permute-start.5
  32.3 2.3 %collective-permute-done.6 = bf16[80,384]{1,0:T(8,128)(2,1)S(1)} collective-permute-done((bf16[80,384]{1,0:T(8,128)(2,1)S(1)}, bf16[80,384]{1,0:T(8,128)(2,1)S(1)}, u32[]{:S(2)}, u32[]{:S(2)}) %collective-permute-start.6) | collective-permute-done | bytes 61472 | tf_op jit(solution)/shard_map/ppermute | solution.py:415
  34.7 3.0 %collective-permute-start.7 = (bf16[80,384]{1,0:T(8,128)(2,1)S(1)}, bf16[80,384]{1,0:T(8,128)(2,1)S(1)}, u32[]{:S(2)}, u32[]{:S(2)}) collective-permute-start(bf16[80,384]{1,0:T(8,128)(2,1)S(1)} %add_convert_fusion.1.pair_ref), channel_id=1, source_target_pairs={{0,2},{1,3},{2,0},{3,1},{4,6},{5,7},{6,4},{7,5},{8,10},{9,11},{10,... | collective-permute-start | bytes 184328 | tf_op jit(solution)/shard_map/ppermute | solution.py:415
  37.7 2.4 %collective-permute-done.5 = bf16[96,1024]{1,0:T(8,128)(2,1)S(1)} collective-permute-done((bf16[96,1024]{1,0:T(8,128)(2,1)S(1)}, bf16[96,1024]{1,0:T(8,128)(2,1)S(1)}, u32[]{:S(2)}, u32[]{:S(2)}) %collective-permute-start.5) | collective-permute-done | bytes 196640 | tf_op jit(solution)/shard_map/ppermute | solution.py:415
  40.1 1.3 %adapter_up.1 = (bf16[96,1024]{1,0:T(8,128)(2,1)S(1)}, bf16[96,1024]{1,0:T(8,128)(2,1)S(1)}, bf16[96,1024]{1,0:T(8,128)(2,1)S(1)}, bf16[96,1024]{1,0:T(8,128)(2,1)S(1)}, f32[96,128]{1,0:T(8,128)S(1)}) custom-call(bf16[80,384]{1,0:T(8,128)(2,1)S(1)} %adapter_down.1.own_ref, bf16[80,384]{1,0:T(8,128)(2,1)S(1)} %add_convert_fusion.1.pair_ref, ...), custom_call_target="tpu_custom_call" | custom-call | flops 805306368 | bytes 2097152 | tf_op jit(solution)/shard_map/adapter_up/pallas_call | solution.py:378
  41.4 0.1 collective-permute-start.9
  41.4 2.8 %collective-permute-start.1 = (bf16[96,1024]{1,0:T(8,128)(2,1)S(1)}, bf16[96,1024]{1,0:T(8,128)(2,1)S(1)}, u32[]{:S(2)}, u32[]{:S(2)}) collective-permute-start(bf16[96,1024]{1,0:T(8,128)(2,1)S(1)} %add_convert_fusion), channel_id=1, source_target_pairs={{0,2},{1,3},{2,0},{3,1},{4,6},{5,7},{6,4},{7,5},{8,10},{9,11},{10,... | collective-permute-start | bytes 589832 | tf_op jit(solution)/shard_map/ppermute | solution.py:415
  44.2 0.2 collective-permute-start.8
  44.4 1.6 %collective-permute-start.10 = (bf16[96,1024]{1,0:T(8,128)(2,1)S(1)}, bf16[96,1024]{1,0:T(8,128)(2,1)S(1)}, u32[]{:S(2)}, u32[]{:S(2)}) collective-permute-start(bf16[96,1024]{1,0:T(8,128)(2,1)S(1)} %add.18), channel_id=1, source_target_pairs={{0,8},{4,12},{8,0},{12,4},{1,9},{5,13},{9,1},{13,5},{2,10},{6,14},... | collective-permute-start | bytes 589832 | tf_op jit(solution)/shard_map/ppermute | solution.py:415
  46.0 0.1 slice_reduce_fusion
  46.1 7.8 %collective-permute-done.1.mid_ref = bf16[96,1024]{1,0:T(8,128)(2,1)S(1)} collective-permute-done((bf16[96,1024]{1,0:T(8,128)(2,1)S(1)}, bf16[96,1024]{1,0:T(8,128)(2,1)S(1)}, u32[]{:S(2)}, u32[]{:S(2)}) %collective-permute-start.1) | collective-permute-done | bytes 196640 | tf_op jit(solution)/shard_map/ppermute | solution.py:415
  53.9 0.1 sum_parts.1
  54.0 0.8 %multiply_convert_fusion = bf16[96,1024]{1,0:T(8,128)(2,1)} fusion(bf16[96,1024]{1,0:T(8,128)(2,1)S(1)} %collective-permute-done.10, f32[96,1024]{1,0:T(8,128)S(1)} %sum_parts.1, bf16[96,1024]{1,0:T(8,128)(2,1)S(1)} %collective-permute-done.5, f32[96]{0:T(128)S(1)} %slice_reduce_fusion), kind=kLoop, calls=%fused_computation | loop fusion | flops 589824 | bytes 983424 | tf_op jit(solution)/shard_map/convert_element_type | solution.py:478
  (13 shorter events, 0.1 us)
Async XLA Ops:
  13.4 12.6 %collective-permute-start.3 = (bf16[96,2176]{1,0:T(8,128)(2,1)S(1)}, bf16[96,2176]{1,0:T(8,128)(2,1)S(1)}, u32[]{:S(2)}, u32[]{:S(2)}) collective-permute-start(bf16[96,2176]{1,0:T(8,128)(2,1)S(1)} %get-tuple-element.21.u_ref.refs_0_), channel_id=1, source_target_pairs={{0,8},{4,12},{8,0},{12,4},{1,9},{5,13},{9,1},{13,5},{2,10},{6,14},... | collective-permute-start | bytes 1253384 | tf_op jit(solution)/shard_map/ppermute | solution.py:415
  16.4 10.1 %collective-permute-start.2 = (bf16[96,2176]{1,0:T(8,128)(2,1)S(1)}, bf16[96,2176]{1,0:T(8,128)(2,1)S(1)}, u32[]{:S(2)}, u32[]{:S(2)}) collective-permute-start(bf16[96,2176]{1,0:T(8,128)(2,1)S(1)} %get-tuple-element.21.u_ref.refs_0_), channel_id=1, source_target_pairs={{0,4},{4,0},{8,12},{12,8},{1,5},{5,1},{9,13},{13,9},{2,6},{6,2},{1... | collective-permute-start | bytes 1253384 | tf_op jit(solution)/shard_map/ppermute | solution.py:415
  19.0 8.9 %copy-start = (bf16[16,2048,64]{1,2,0:T(8,128)(2,1)S(1)}, bf16[16,2048,64]{1,2,0:T(8,128)(2,1)}, u32[]{:S(2)}) copy-start(bf16[16,2048,64]{1,2,0:T(8,128)(2,1)} %param.26) | copy-start | bytes 12582916
  19.0 21.1 %copy-start.1 = (bf16[16,64,1024]{2,1,0:T(8,128)(2,1)S(1)}, bf16[16,64,1024]{2,1,0:T(8,128)(2,1)}, u32[]{:S(2)}) copy-start(bf16[16,64,1024]{2,1,0:T(8,128)(2,1)} %param.27) | copy-start | bytes 6291460
  19.0 7.5 %collective-permute-start = (bf16[96,1024]{1,0:T(8,128)(2,1)S(1)}, bf16[96,1024]{1,0:T(8,128)(2,1)S(1)}, u32[]{:S(2)}, u32[]{:S(2)}) collective-permute-start(bf16[96,1024]{1,0:T(8,128)(2,1)S(1)} %base_first.1), channel_id=1, source_target_pairs={{0,1},{1,0},{2,3},{3,2},{4,5},{5,4},{6,7},{7,6},{8,9},{9,8},{10,11... | collective-permute-start | bytes 589832 | tf_op jit(solution)/shard_map/ppermute | solution.py:415
  26.1 1.8 %collective-permute-start.4 = (bf16[96,2176]{1,0:T(8,128)(2,1)S(1)}, bf16[96,2176]{1,0:T(8,128)(2,1)S(1)}, u32[]{:S(2)}, u32[]{:S(2)}) collective-permute-start(bf16[96,2176]{1,0:T(8,128)(2,1)S(1)} %collective-permute-done.3.refs_2_), channel_id=1, source_target_pairs={{0,4},{4,0},{8,12},{12,8},{1,5},{5,1},{9,13},{13,9},{2,6},{6,2},{1... | collective-permute-start | bytes 1253384 | tf_op jit(solution)/shard_map/ppermute | solution.py:415
  30.2 4.4 %collective-permute-start.6 = (bf16[80,384]{1,0:T(8,128)(2,1)S(1)}, bf16[80,384]{1,0:T(8,128)(2,1)S(1)}, u32[]{:S(2)}, u32[]{:S(2)}) collective-permute-start(bf16[80,384]{1,0:T(8,128)(2,1)S(1)} %adapter_down.1.own_ref), channel_id=1, source_target_pairs={{0,1},{1,0},{2,3},{3,2},{4,5},{5,4},{6,7},{7,6},{8,9},{9,8},{10,11... | collective-permute-start | bytes 184328 | tf_op jit(solution)/shard_map/ppermute | solution.py:415
  32.1 8.0 %collective-permute-start.5 = (bf16[96,1024]{1,0:T(8,128)(2,1)S(1)}, bf16[96,1024]{1,0:T(8,128)(2,1)S(1)}, u32[]{:S(2)}, u32[]{:S(2)}) collective-permute-start(bf16[96,1024]{1,0:T(8,128)(2,1)S(1)} %get-tuple-element.24), channel_id=1, source_target_pairs={{0,1},{1,0},{2,3},{3,2},{4,5},{5,4},{6,7},{7,6},{8,9},{9,8},{10,11... | collective-permute-start | bytes 589832 | tf_op jit(solution)/shard_map/ppermute | solution.py:415
  34.7 5.4 %collective-permute-start.7 = (bf16[80,384]{1,0:T(8,128)(2,1)S(1)}, bf16[80,384]{1,0:T(8,128)(2,1)S(1)}, u32[]{:S(2)}, u32[]{:S(2)}) collective-permute-start(bf16[80,384]{1,0:T(8,128)(2,1)S(1)} %add_convert_fusion.1.pair_ref), channel_id=1, source_target_pairs={{0,2},{1,3},{2,0},{3,1},{4,6},{5,7},{6,4},{7,5},{8,10},{9,11},{10,... | collective-permute-start | bytes 184328 | tf_op jit(solution)/shard_map/ppermute | solution.py:415
  41.4 3.0 %collective-permute-start.9 = (bf16[96,1024]{1,0:T(8,128)(2,1)S(1)}, bf16[96,1024]{1,0:T(8,128)(2,1)S(1)}, u32[]{:S(2)}, u32[]{:S(2)}) collective-permute-start(bf16[96,1024]{1,0:T(8,128)(2,1)S(1)} %get-tuple-element.29), channel_id=1, source_target_pairs={{0,4},{4,0},{8,12},{12,8},{1,5},{5,1},{9,13},{13,9},{2,6},{6,2},{1... | collective-permute-start | bytes 589832 | tf_op jit(solution)/shard_map/ppermute | solution.py:415
  41.4 12.5 %collective-permute-start.1 = (bf16[96,1024]{1,0:T(8,128)(2,1)S(1)}, bf16[96,1024]{1,0:T(8,128)(2,1)S(1)}, u32[]{:S(2)}, u32[]{:S(2)}) collective-permute-start(bf16[96,1024]{1,0:T(8,128)(2,1)S(1)} %add_convert_fusion), channel_id=1, source_target_pairs={{0,2},{1,3},{2,0},{3,1},{4,6},{5,7},{6,4},{7,5},{8,10},{9,11},{10,... | collective-permute-start | bytes 589832 | tf_op jit(solution)/shard_map/ppermute | solution.py:415
  44.2 9.7 %collective-permute-start.8 = (bf16[96,1024]{1,0:T(8,128)(2,1)S(1)}, bf16[96,1024]{1,0:T(8,128)(2,1)S(1)}, u32[]{:S(2)}, u32[]{:S(2)}) collective-permute-start(bf16[96,1024]{1,0:T(8,128)(2,1)S(1)} %get-tuple-element.27), channel_id=1, source_target_pairs={{0,4},{4,0},{8,12},{12,8},{1,5},{5,1},{9,13},{13,9},{2,6},{6,2},{1... | collective-permute-start | bytes 589832 | tf_op jit(solution)/shard_map/ppermute | solution.py:415
  44.4 9.6 %collective-permute-start.10 = (bf16[96,1024]{1,0:T(8,128)(2,1)S(1)}, bf16[96,1024]{1,0:T(8,128)(2,1)S(1)}, u32[]{:S(2)}, u32[]{:S(2)}) collective-permute-start(bf16[96,1024]{1,0:T(8,128)(2,1)S(1)} %add.18), channel_id=1, source_target_pairs={{0,8},{4,12},{8,0},{12,4},{1,9},{5,13},{9,1},{13,5},{2,10},{6,14},... | collective-permute-start | bytes 589832 | tf_op jit(solution)/shard_map/ppermute | solution.py:415

commit v4 on v3

--- a/solution.py
+++ b/solution.py
@@ -151,19 +151,20 @@
             out_rows.append(gated * gain)
         u_ref[:, columns(c)] = jnp.concatenate(out_rows, axis=0).astype(BF)
 
-    for i in (0, 1, 5, 8, 9):
+    copies[0].wait()
+    scaled_inputs(0)
+    for i in (1, 5, 8, 9):
         copies[i].wait()
-    scaled_inputs(0)
     z_ref[...] = jnp.zeros_like(z_ref)
 
     def chunk(c, carry):
         state_in(c).wait()
         xet = xet_ref[lax.rem(c, 2)]
-        z = jnp.zeros((tr, cols), F32)
+        z = jnp.zeros((cols, tr), F32)
         for p in range(pairs):
             s0 = s_buf[2 * p, pl.ds(c * hb, hb)].reshape(cols, n)
             s1 = s_buf[2 * p + 1, pl.ds(c * hb, hb)].reshape(cols, n)
-            z = z + dot(qbd_ref[p], jnp.concatenate([s0, s1], axis=1), NT)
+            z = z + dot(jnp.concatenate([s0, s1], axis=1), qbd_ref[p], NT)
             up = dot(xet, wbd_ref[p])
             for half, sv in ((0, s0), (1, s1)):
                 r = 2 * p + half
@@ -175,7 +176,7 @@
                 o_buf[r, pl.ds(c * hb, hb)] = grown.astype(BF)
         scaled_inputs(jnp.minimum(c + 1, chunks - 1))
         gated_rows(jnp.maximum(c - 1, 0))
-        z_ref[lax.rem(c, 2)] = z
+        z_ref[lax.rem(c, 2)] = z.T
         state_out(c).start()
         return carry
 

time: 55 us -> 54.3 us (0.987)
  Pallas kernels: 24.3 us -> 23.6 us
    pallas_call x1, Pallas kernels: 12.8 us -> 12.1 us  [state_call(): pl.pallas_call(functools.partial(state_body, hb), in_specs=[ANY] * len(op...]
  transfers between devices with their start and end apart: 11 -> 11, of which waited for: 5 -> 5; matrix products, arithmetic and copies ran while one was open for 0% -> 0% of each run, Pallas kernels for 14% -> 15%
where the time goes in v4:
time: 54.3 us; the launch traced here: 54.2 us
  Pallas kernels  23.6 us (43%)
  starting transfers between devices  14.7 us (27%)
  waiting for transfers between devices  14.1 us (26%)
  other arithmetic  0.88 us (2%)
  between operations  0.75 us (1%)
    ppermute x11, starting transfers between devices, swap(): return lax.ppermute(a, axis, [(i, i ^ bit) for i in range(size)])  14.7 us
    ppermute x11, waiting for transfers between devices, swap(): return lax.ppermute(a, axis, [(i, i ^ bit) for i in range(size)])  14.1 us
    pallas_call x1, Pallas kernels, state_call(): pl.pallas_call(functools.partial(state_body, hb), in_specs=[ANY] * len(op...  12.1 us
    pallas_call x2, Pallas kernels, base_call(): pl.pallas_call(functools.partial(base_body, flips, features), in_specs=[V...  7.77 us
    pallas_call x1, Pallas kernels, down_call(): pl.pallas_call(functools.partial(down_body, sources, rank), in_specs=[VM]...  2.35 us
    pallas_call x1, Pallas kernels, up_call(): pl.pallas_call(functools.partial(up_body, rank, width), in_specs=[VM] * 4...  1.25 us
  transfers between devices with their start and end apart: 11, of which 5 were waited for; matrix products, arithmetic and copies ran while one was open for 0% of the time, Pallas kernels for 15%

profile of v4, /device:TPU:0, one launch (start us, length us, event | category | flops | bytes accessed | tf_op | source)
XLA Modules:
  0.0 54.2 jit_solution(4889818280773857748)
XLA Ops:
  0.6 12.1 %state_steps.1 = (bf16[24,32,64,128]{3,2,1,0:T(8,128)(2,1)}, bf16[96,2176]{1,0:T(8,128)(2,1)S(1)}, f32[96,128]{1,0:T(8,128)S(1)}) custom-call(bf16[4,24,2048]{2,1,0:T(8,128)(2,1)} %refs_0_.1, bf16[4,24,2048]{2,1,0:T(8,128)(2,1)} %refs_1_.1, f32[4,24,32]{2,1,0:T(8,128)} %refs_2_.1, f32[1,32]{1,0:T(1,128)} %bitcast.12, f32[1,32]{1,0:T(1,128)} %bitcast.13, ...), custom_call_target="tpu_custom_call" | custom-call | flops 2415919104 | bytes 25165824 | tf_op jit(solution)/shard_map/state_steps/pallas_call | solution.py:233
  12.8 3.0 %collective-permute-start.3 = (bf16[96,2176]{1,0:T(8,128)(2,1)S(1)}, bf16[96,2176]{1,0:T(8,128)(2,1)S(1)}, u32[]{:S(2)}, u32[]{:S(2)}) collective-permute-start(bf16[96,2176]{1,0:T(8,128)(2,1)S(1)} %get-tuple-element.21.u_ref.refs_0_), channel_id=1, source_target_pairs={{0,8},{4,12},{8,0},{12,4},{1,9},{5,13},{9,1},{13,5},{2,10},{6,14},... | collective-permute-start | bytes 1253384 | tf_op jit(solution)/shard_map/ppermute | solution.py:416
  15.8 2.5 %base_first.1 = bf16[96,1024]{1,0:T(8,128)(2,1)S(1)} custom-call(bf16[96,2176]{1,0:T(8,128)(2,1)S(1)} %get-tuple-element.21.u_ref.refs_0_, bf16[2048,4096]{1,0:T(8,128)(2,1)} %w_ref.3), custom_call_target="tpu_custom_call" | custom-call | flops 402653184 | bytes 4194304 | tf_op jit(solution)/shard_map/base_first/pallas_call | solution.py:284
  18.3 0.0 copy-start
  18.3 1.6 %collective-permute-start = (bf16[96,1024]{1,0:T(8,128)(2,1)S(1)}, bf16[96,1024]{1,0:T(8,128)(2,1)S(1)}, u32[]{:S(2)}, u32[]{:S(2)}) collective-permute-start(bf16[96,1024]{1,0:T(8,128)(2,1)S(1)} %base_first.1), channel_id=1, source_target_pairs={{0,1},{1,0},{2,3},{3,2},{4,5},{5,4},{6,7},{7,6},{8,9},{9,8},{10,11... | collective-permute-start | bytes 589832 | tf_op jit(solution)/shard_map/ppermute | solution.py:416
  20.0 5.2 %base_rest.1 = (f32[96,1024]{1,0:T(8,128)S(1)}, bf16[96,1024]{1,0:T(8,128)(2,1)S(1)}, f32[96,1024]{1,0:T(8,128)S(1)}) custom-call(bf16[96,2176]{1,0:T(8,128)(2,1)S(1)} %get-tuple-element.21.u_ref.refs_0_, bf16[2048,4096]{1,0:T(8,128)(2,1)} %w_ref.3), custom_call_target="tpu_custom_call" | custom-call | flops 1207959552 | bytes 12582912 | tf_op jit(solution)/shard_map/base_rest/pallas_call | solution.py:284
  25.2 0.2 collective-permute-done.3.refs_2_
  25.4 0.4 collective-permute-start.4
  25.9 1.3 %collective-permute-done.4.refs_3_ = bf16[96,2176]{1,0:T(8,128)(2,1)S(1)} collective-permute-done((bf16[96,2176]{1,0:T(8,128)(2,1)S(1)}, bf16[96,2176]{1,0:T(8,128)(2,1)S(1)}, u32[]{:S(2)}, u32[]{:S(2)}) %collective-permute-start.4) | collective-permute-done | bytes 417824 | tf_op jit(solution)/shard_map/ppermute | solution.py:416
  27.2 2.4 %adapter_down.1.own_ref = bf16[80,384]{1,0:T(8,128)(2,1)S(1)} custom-call(bf16[96,2176]{1,0:T(8,128)(2,1)S(1)} %get-tuple-element.21.u_ref.refs_0_, bf16[96,2176]{1,0:T(8,128)(2,1)S(1)} %collective-permute-done.2.refs_1_, bf16[96,2176]{1,0:T(8,128)(2,1)S(1)} %collective-permute-done.3.refs_2_, bf16[96,2176]{1,0:T(8,128)(2,1)S(1)} %collective-permute-done.4.refs_3_, ...), custom_call_target="tpu_custom_call" | custom-call | flops 1610612736 | bytes 4194304 | tf_op jit(solution)/shard_map/adapter_down/pallas_call | solution.py:338
  29.6 1.9 %collective-permute-start.6 = (bf16[80,384]{1,0:T(8,128)(2,1)S(1)}, bf16[80,384]{1,0:T(8,128)(2,1)S(1)}, u32[]{:S(2)}, u32[]{:S(2)}) collective-permute-start(bf16[80,384]{1,0:T(8,128)(2,1)S(1)} %adapter_down.1.own_ref), channel_id=1, source_target_pairs={{0,1},{1,0},{2,3},{3,2},{4,5},{5,4},{6,7},{7,6},{8,9},{9,8},{10,11... | collective-permute-start | bytes 184328 | tf_op jit(solution)/shard_map/ppermute | solution.py:416
  31.4 0.2 collective-permute-start.5
  31.7 2.3 %collective-permute-done.6 = bf16[80,384]{1,0:T(8,128)(2,1)S(1)} collective-permute-done((bf16[80,384]{1,0:T(8,128)(2,1)S(1)}, bf16[80,384]{1,0:T(8,128)(2,1)S(1)}, u32[]{:S(2)}, u32[]{:S(2)}) %collective-permute-start.6) | collective-permute-done | bytes 61472 | tf_op jit(solution)/shard_map/ppermute | solution.py:416
  34.0 3.0 %collective-permute-start.7 = (bf16[80,384]{1,0:T(8,128)(2,1)S(1)}, bf16[80,384]{1,0:T(8,128)(2,1)S(1)}, u32[]{:S(2)}, u32[]{:S(2)}) collective-permute-start(bf16[80,384]{1,0:T(8,128)(2,1)S(1)} %add_convert_fusion.1.pair_ref), channel_id=1, source_target_pairs={{0,2},{1,3},{2,0},{3,1},{4,6},{5,7},{6,4},{7,5},{8,10},{9,11},{10,... | collective-permute-start | bytes 184328 | tf_op jit(solution)/shard_map/ppermute | solution.py:416
  37.0 2.4 %collective-permute-done.5 = bf16[96,1024]{1,0:T(8,128)(2,1)S(1)} collective-permute-done((bf16[96,1024]{1,0:T(8,128)(2,1)S(1)}, bf16[96,1024]{1,0:T(8,128)(2,1)S(1)}, u32[]{:S(2)}, u32[]{:S(2)}) %collective-permute-start.5) | collective-permute-done | bytes 196640 | tf_op jit(solution)/shard_map/ppermute | solution.py:416
  39.4 1.3 %adapter_up.1 = (bf16[96,1024]{1,0:T(8,128)(2,1)S(1)}, bf16[96,1024]{1,0:T(8,128)(2,1)S(1)}, bf16[96,1024]{1,0:T(8,128)(2,1)S(1)}, bf16[96,1024]{1,0:T(8,128)(2,1)S(1)}, f32[96,128]{1,0:T(8,128)S(1)}) custom-call(bf16[80,384]{1,0:T(8,128)(2,1)S(1)} %adapter_down.1.own_ref, bf16[80,384]{1,0:T(8,128)(2,1)S(1)} %add_convert_fusion.1.pair_ref, ...), custom_call_target="tpu_custom_call" | custom-call | flops 805306368 | bytes 2097152 | tf_op jit(solution)/shard_map/adapter_up/pallas_call | solution.py:379
  40.7 0.1 collective-permute-start.9
  40.8 2.8 %collective-permute-start.1 = (bf16[96,1024]{1,0:T(8,128)(2,1)S(1)}, bf16[96,1024]{1,0:T(8,128)(2,1)S(1)}, u32[]{:S(2)}, u32[]{:S(2)}) collective-permute-start(bf16[96,1024]{1,0:T(8,128)(2,1)S(1)} %add_convert_fusion), channel_id=1, source_target_pairs={{0,2},{1,3},{2,0},{3,1},{4,6},{5,7},{6,4},{7,5},{8,10},{9,11},{10,... | collective-permute-start | bytes 589832 | tf_op jit(solution)/shard_map/ppermute | solution.py:416
  43.6 0.2 collective-permute-start.8
  43.8 1.5 %collective-permute-start.10 = (bf16[96,1024]{1,0:T(8,128)(2,1)S(1)}, bf16[96,1024]{1,0:T(8,128)(2,1)S(1)}, u32[]{:S(2)}, u32[]{:S(2)}) collective-permute-start(bf16[96,1024]{1,0:T(8,128)(2,1)S(1)} %add.18), channel_id=1, source_target_pairs={{0,8},{4,12},{8,0},{12,4},{1,9},{5,13},{9,1},{13,5},{2,10},{6,14},... | collective-permute-start | bytes 589832 | tf_op jit(solution)/shard_map/ppermute | solution.py:416
  45.3 0.1 slice_reduce_fusion
  45.4 7.8 %collective-permute-done.1.mid_ref = bf16[96,1024]{1,0:T(8,128)(2,1)S(1)} collective-permute-done((bf16[96,1024]{1,0:T(8,128)(2,1)S(1)}, bf16[96,1024]{1,0:T(8,128)(2,1)S(1)}, u32[]{:S(2)}, u32[]{:S(2)}) %collective-permute-start.1) | collective-permute-done | bytes 196640 | tf_op jit(solution)/shard_map/ppermute | solution.py:416
  53.3 0.1 sum_parts.1
  53.4 0.8 %multiply_convert_fusion = bf16[96,1024]{1,0:T(8,128)(2,1)} fusion(bf16[96,1024]{1,0:T(8,128)(2,1)S(1)} %collective-permute-done.10, f32[96,1024]{1,0:T(8,128)S(1)} %sum_parts.1, bf16[96,1024]{1,0:T(8,128)(2,1)S(1)} %collective-permute-done.5, f32[96]{0:T(128)S(1)} %slice_reduce_fusion), kind=kLoop, calls=%fused_computation | loop fusion | flops 589824 | bytes 983424 | tf_op jit(solution)/shard_map/convert_element_type | solution.py:479
  (13 shorter events, 0.1 us)
Async XLA Ops:
  12.8 12.7 %collective-permute-start.3 = (bf16[96,2176]{1,0:T(8,128)(2,1)S(1)}, bf16[96,2176]{1,0:T(8,128)(2,1)S(1)}, u32[]{:S(2)}, u32[]{:S(2)}) collective-permute-start(bf16[96,2176]{1,0:T(8,128)(2,1)S(1)} %get-tuple-element.21.u_ref.refs_0_), channel_id=1, source_target_pairs={{0,8},{4,12},{8,0},{12,4},{1,9},{5,13},{9,1},{13,5},{2,10},{6,14},... | collective-permute-start | bytes 1253384 | tf_op jit(solution)/shard_map/ppermute | solution.py:416
  15.8 10.1 %collective-permute-start.2 = (bf16[96,2176]{1,0:T(8,128)(2,1)S(1)}, bf16[96,2176]{1,0:T(8,128)(2,1)S(1)}, u32[]{:S(2)}, u32[]{:S(2)}) collective-permute-start(bf16[96,2176]{1,0:T(8,128)(2,1)S(1)} %get-tuple-element.21.u_ref.refs_0_), channel_id=1, source_target_pairs={{0,4},{4,0},{8,12},{12,8},{1,5},{5,1},{9,13},{13,9},{2,6},{6,2},{1... | collective-permute-start | bytes 1253384 | tf_op jit(solution)/shard_map/ppermute | solution.py:416
  18.3 8.9 %copy-start = (bf16[16,2048,64]{1,2,0:T(8,128)(2,1)S(1)}, bf16[16,2048,64]{1,2,0:T(8,128)(2,1)}, u32[]{:S(2)}) copy-start(bf16[16,2048,64]{1,2,0:T(8,128)(2,1)} %param.26) | copy-start | bytes 12582916
  18.3 21.1 %copy-start.1 = (bf16[16,64,1024]{2,1,0:T(8,128)(2,1)S(1)}, bf16[16,64,1024]{2,1,0:T(8,128)(2,1)}, u32[]{:S(2)}) copy-start(bf16[16,64,1024]{2,1,0:T(8,128)(2,1)} %param.27) | copy-start | bytes 6291460
  18.3 7.5 %collective-permute-start = (bf16[96,1024]{1,0:T(8,128)(2,1)S(1)}, bf16[96,1024]{1,0:T(8,128)(2,1)S(1)}, u32[]{:S(2)}, u32[]{:S(2)}) collective-permute-start(bf16[96,1024]{1,0:T(8,128)(2,1)S(1)} %base_first.1), channel_id=1, source_target_pairs={{0,1},{1,0},{2,3},{3,2},{4,5},{5,4},{6,7},{7,6},{8,9},{9,8},{10,11... | collective-permute-start | bytes 589832 | tf_op jit(solution)/shard_map/ppermute | solution.py:416
  25.4 1.8 %collective-permute-start.4 = (bf16[96,2176]{1,0:T(8,128)(2,1)S(1)}, bf16[96,2176]{1,0:T(8,128)(2,1)S(1)}, u32[]{:S(2)}, u32[]{:S(2)}) collective-permute-start(bf16[96,2176]{1,0:T(8,128)(2,1)S(1)} %collective-permute-done.3.refs_2_), channel_id=1, source_target_pairs={{0,4},{4,0},{8,12},{12,8},{1,5},{5,1},{9,13},{13,9},{2,6},{6,2},{1... | collective-permute-start | bytes 1253384 | tf_op jit(solution)/shard_map/ppermute | solution.py:416
  29.6 4.4 %collective-permute-start.6 = (bf16[80,384]{1,0:T(8,128)(2,1)S(1)}, bf16[80,384]{1,0:T(8,128)(2,1)S(1)}, u32[]{:S(2)}, u32[]{:S(2)}) collective-permute-start(bf16[80,384]{1,0:T(8,128)(2,1)S(1)} %adapter_down.1.own_ref), channel_id=1, source_target_pairs={{0,1},{1,0},{2,3},{3,2},{4,5},{5,4},{6,7},{7,6},{8,9},{9,8},{10,11... | collective-permute-start | bytes 184328 | tf_op jit(solution)/shard_map/ppermute | solution.py:416
  31.4 8.0 %collective-permute-start.5 = (bf16[96,1024]{1,0:T(8,128)(2,1)S(1)}, bf16[96,1024]{1,0:T(8,128)(2,1)S(1)}, u32[]{:S(2)}, u32[]{:S(2)}) collective-permute-start(bf16[96,1024]{1,0:T(8,128)(2,1)S(1)} %get-tuple-element.24), channel_id=1, source_target_pairs={{0,1},{1,0},{2,3},{3,2},{4,5},{5,4},{6,7},{7,6},{8,9},{9,8},{10,11... | collective-permute-start | bytes 589832 | tf_op jit(solution)/shard_map/ppermute | solution.py:416
  34.0 5.4 %collective-permute-start.7 = (bf16[80,384]{1,0:T(8,128)(2,1)S(1)}, bf16[80,384]{1,0:T(8,128)(2,1)S(1)}, u32[]{:S(2)}, u32[]{:S(2)}) collective-permute-start(bf16[80,384]{1,0:T(8,128)(2,1)S(1)} %add_convert_fusion.1.pair_ref), channel_id=1, source_target_pairs={{0,2},{1,3},{2,0},{3,1},{4,6},{5,7},{6,4},{7,5},{8,10},{9,11},{10,... | collective-permute-start | bytes 184328 | tf_op jit(solution)/shard_map/ppermute | solution.py:416
  40.7 3.0 %collective-permute-start.9 = (bf16[96,1024]{1,0:T(8,128)(2,1)S(1)}, bf16[96,1024]{1,0:T(8,128)(2,1)S(1)}, u32[]{:S(2)}, u32[]{:S(2)}) collective-permute-start(bf16[96,1024]{1,0:T(8,128)(2,1)S(1)} %get-tuple-element.29), channel_id=1, source_target_pairs={{0,4},{4,0},{8,12},{12,8},{1,5},{5,1},{9,13},{13,9},{2,6},{6,2},{1... | collective-permute-start | bytes 589832 | tf_op jit(solution)/shard_map/ppermute | solution.py:416
  40.8 12.5 %collective-permute-start.1 = (bf16[96,1024]{1,0:T(8,128)(2,1)S(1)}, bf16[96,1024]{1,0:T(8,128)(2,1)S(1)}, u32[]{:S(2)}, u32[]{:S(2)}) collective-permute-start(bf16[96,1024]{1,0:T(8,128)(2,1)S(1)} %add_convert_fusion), channel_id=1, source_target_pairs={{0,2},{1,3},{2,0},{3,1},{4,6},{5,7},{6,4},{7,5},{8,10},{9,11},{10,... | collective-permute-start | bytes 589832 | tf_op jit(solution)/shard_map/ppermute | solution.py:416
  43.6 9.7 %collective-permute-start.8 = (bf16[96,1024]{1,0:T(8,128)(2,1)S(1)}, bf16[96,1024]{1,0:T(8,128)(2,1)S(1)}, u32[]{:S(2)}, u32[]{:S(2)}) collective-permute-start(bf16[96,1024]{1,0:T(8,128)(2,1)S(1)} %get-tuple-element.27), channel_id=1, source_target_pairs={{0,4},{4,0},{8,12},{12,8},{1,5},{5,1},{9,13},{13,9},{2,6},{6,2},{1... | collective-permute-start | bytes 589832 | tf_op jit(solution)/shard_map/ppermute | solution.py:416
  43.8 9.6 %collective-permute-start.10 = (bf16[96,1024]{1,0:T(8,128)(2,1)S(1)}, bf16[96,1024]{1,0:T(8,128)(2,1)S(1)}, u32[]{:S(2)}, u32[]{:S(2)}) collective-permute-start(bf16[96,1024]{1,0:T(8,128)(2,1)S(1)} %add.18), channel_id=1, source_target_pairs={{0,8},{4,12},{8,0},{12,4},{1,9},{5,13},{9,1},{13,5},{2,10},{6,14},... | collective-permute-start | bytes 589832 | tf_op jit(solution)/shard_map/ppermute | solution.py:416

commit v5 on v4

--- a/solution.py
+++ b/solution.py
@@ -174,10 +174,10 @@
                     + up[:, half * n : (half + 1) * n].reshape(hb, HEAD_WIDTH, n)
                 )
                 o_buf[r, pl.ds(c * hb, hb)] = grown.astype(BF)
+        state_out(c).start()
         scaled_inputs(jnp.minimum(c + 1, chunks - 1))
         gated_rows(jnp.maximum(c - 1, 0))
         z_ref[lax.rem(c, 2)] = z.T
-        state_out(c).start()
         return carry
 
     lax.fori_loop(0, chunks, chunk, 0)

time: 54.3 us -> 54.3 us (level)
  no operation moved by 1% of the time
where the time goes in v5:
time: 54.3 us; the launch traced here: 54.2 us
  Pallas kernels  23.6 us (43%)
  starting transfers between devices  14.7 us (27%)
  waiting for transfers between devices  14.1 us (26%)
  other arithmetic  0.88 us (2%)
  between operations  0.75 us (1%)
    ppermute x11, starting transfers between devices, swap(): return lax.ppermute(a, axis, [(i, i ^ bit) for i in range(size)])  14.7 us
    ppermute x11, waiting for transfers between devices, swap(): return lax.ppermute(a, axis, [(i, i ^ bit) for i in range(size)])  14.1 us
    pallas_call x1, Pallas kernels, state_call(): pl.pallas_call(functools.partial(state_body, hb), in_specs=[ANY] * len(op...  12.1 us
    pallas_call x2, Pallas kernels, base_call(): pl.pallas_call(functools.partial(base_body, flips, features), in_specs=[V...  7.77 us
    pallas_call x1, Pallas kernels, down_call(): pl.pallas_call(functools.partial(down_body, sources, rank), in_specs=[VM]...  2.35 us
    pallas_call x1, Pallas kernels, up_call(): pl.pallas_call(functools.partial(up_body, rank, width), in_specs=[VM] * 4...  1.25 us
  transfers between devices with their start and end apart: 11, of which 5 were waited for; matrix products, arithmetic and copies ran while one was open for 0% of the time, Pallas kernels for 15%

profile of v5, /device:TPU:0, one launch (start us, length us, event | category | flops | bytes accessed | tf_op | source)
XLA Modules:
  0.0 54.2 jit_solution(4889818280773857748)
XLA Ops:
  0.6 12.1 %state_steps.1 = (bf16[24,32,64,128]{3,2,1,0:T(8,128)(2,1)}, bf16[96,2176]{1,0:T(8,128)(2,1)S(1)}, f32[96,128]{1,0:T(8,128)S(1)}) custom-call(bf16[4,24,2048]{2,1,0:T(8,128)(2,1)} %refs_0_.1, bf16[4,24,2048]{2,1,0:T(8,128)(2,1)} %refs_1_.1, f32[4,24,32]{2,1,0:T(8,128)} %refs_2_.1, f32[1,32]{1,0:T(1,128)} %bitcast.12, f32[1,32]{1,0:T(1,128)} %bitcast.13, ...), custom_call_target="tpu_custom_call" | custom-call | flops 2415919104 | bytes 25165824 | tf_op jit(solution)/shard_map/state_steps/pallas_call | solution.py:233
  12.8 3.0 %collective-permute-start.3 = (bf16[96,2176]{1,0:T(8,128)(2,1)S(1)}, bf16[96,2176]{1,0:T(8,128)(2,1)S(1)}, u32[]{:S(2)}, u32[]{:S(2)}) collective-permute-start(bf16[96,2176]{1,0:T(8,128)(2,1)S(1)} %get-tuple-element.21.u_ref.refs_0_), channel_id=1, source_target_pairs={{0,8},{4,12},{8,0},{12,4},{1,9},{5,13},{9,1},{13,5},{2,10},{6,14},... | collective-permute-start | bytes 1253384 | tf_op jit(solution)/shard_map/ppermute | solution.py:416
  15.8 2.5 %base_first.1 = bf16[96,1024]{1,0:T(8,128)(2,1)S(1)} custom-call(bf16[96,2176]{1,0:T(8,128)(2,1)S(1)} %get-tuple-element.21.u_ref.refs_0_, bf16[2048,4096]{1,0:T(8,128)(2,1)} %w_ref.3), custom_call_target="tpu_custom_call" | custom-call | flops 402653184 | bytes 4194304 | tf_op jit(solution)/shard_map/base_first/pallas_call | solution.py:284
  18.3 0.0 copy-start
  18.3 1.6 %collective-permute-start = (bf16[96,1024]{1,0:T(8,128)(2,1)S(1)}, bf16[96,1024]{1,0:T(8,128)(2,1)S(1)}, u32[]{:S(2)}, u32[]{:S(2)}) collective-permute-start(bf16[96,1024]{1,0:T(8,128)(2,1)S(1)} %base_first.1), channel_id=1, source_target_pairs={{0,1},{1,0},{2,3},{3,2},{4,5},{5,4},{6,7},{7,6},{8,9},{9,8},{10,11... | collective-permute-start | bytes 589832 | tf_op jit(solution)/shard_map/ppermute | solution.py:416
  20.0 5.2 %base_rest.1 = (f32[96,1024]{1,0:T(8,128)S(1)}, bf16[96,1024]{1,0:T(8,128)(2,1)S(1)}, f32[96,1024]{1,0:T(8,128)S(1)}) custom-call(bf16[96,2176]{1,0:T(8,128)(2,1)S(1)} %get-tuple-element.21.u_ref.refs_0_, bf16[2048,4096]{1,0:T(8,128)(2,1)} %w_ref.3), custom_call_target="tpu_custom_call" | custom-call | flops 1207959552 | bytes 12582912 | tf_op jit(solution)/shard_map/base_rest/pallas_call | solution.py:284
  25.2 0.2 collective-permute-done.3.refs_2_
  25.4 0.4 collective-permute-start.4
  25.9 1.3 %collective-permute-done.4.refs_3_ = bf16[96,2176]{1,0:T(8,128)(2,1)S(1)} collective-permute-done((bf16[96,2176]{1,0:T(8,128)(2,1)S(1)}, bf16[96,2176]{1,0:T(8,128)(2,1)S(1)}, u32[]{:S(2)}, u32[]{:S(2)}) %collective-permute-start.4) | collective-permute-done | bytes 417824 | tf_op jit(solution)/shard_map/ppermute | solution.py:416
  27.2 2.4 %adapter_down.1.own_ref = bf16[80,384]{1,0:T(8,128)(2,1)S(1)} custom-call(bf16[96,2176]{1,0:T(8,128)(2,1)S(1)} %get-tuple-element.21.u_ref.refs_0_, bf16[96,2176]{1,0:T(8,128)(2,1)S(1)} %collective-permute-done.2.refs_1_, bf16[96,2176]{1,0:T(8,128)(2,1)S(1)} %collective-permute-done.3.refs_2_, bf16[96,2176]{1,0:T(8,128)(2,1)S(1)} %collective-permute-done.4.refs_3_, ...), custom_call_target="tpu_custom_call" | custom-call | flops 1610612736 | bytes 4194304 | tf_op jit(solution)/shard_map/adapter_down/pallas_call | solution.py:338
  29.6 1.9 %collective-permute-start.6 = (bf16[80,384]{1,0:T(8,128)(2,1)S(1)}, bf16[80,384]{1,0:T(8,128)(2,1)S(1)}, u32[]{:S(2)}, u32[]{:S(2)}) collective-permute-start(bf16[80,384]{1,0:T(8,128)(2,1)S(1)} %adapter_down.1.own_ref), channel_id=1, source_target_pairs={{0,1},{1,0},{2,3},{3,2},{4,5},{5,4},{6,7},{7,6},{8,9},{9,8},{10,11... | collective-permute-start | bytes 184328 | tf_op jit(solution)/shard_map/ppermute | solution.py:416
  31.4 0.2 collective-permute-start.5
  31.7 2.3 %collective-permute-done.6 = bf16[80,384]{1,0:T(8,128)(2,1)S(1)} collective-permute-done((bf16[80,384]{1,0:T(8,128)(2,1)S(1)}, bf16[80,384]{1,0:T(8,128)(2,1)S(1)}, u32[]{:S(2)}, u32[]{:S(2)}) %collective-permute-start.6) | collective-permute-done | bytes 61472 | tf_op jit(solution)/shard_map/ppermute | solution.py:416
  34.0 3.0 %collective-permute-start.7 = (bf16[80,384]{1,0:T(8,128)(2,1)S(1)}, bf16[80,384]{1,0:T(8,128)(2,1)S(1)}, u32[]{:S(2)}, u32[]{:S(2)}) collective-permute-start(bf16[80,384]{1,0:T(8,128)(2,1)S(1)} %add_convert_fusion.1.pair_ref), channel_id=1, source_target_pairs={{0,2},{1,3},{2,0},{3,1},{4,6},{5,7},{6,4},{7,5},{8,10},{9,11},{10,... | collective-permute-start | bytes 184328 | tf_op jit(solution)/shard_map/ppermute | solution.py:416
  37.0 2.4 %collective-permute-done.5 = bf16[96,1024]{1,0:T(8,128)(2,1)S(1)} collective-permute-done((bf16[96,1024]{1,0:T(8,128)(2,1)S(1)}, bf16[96,1024]{1,0:T(8,128)(2,1)S(1)}, u32[]{:S(2)}, u32[]{:S(2)}) %collective-permute-start.5) | collective-permute-done | bytes 196640 | tf_op jit(solution)/shard_map/ppermute | solution.py:416
  39.4 1.3 %adapter_up.1 = (bf16[96,1024]{1,0:T(8,128)(2,1)S(1)}, bf16[96,1024]{1,0:T(8,128)(2,1)S(1)}, bf16[96,1024]{1,0:T(8,128)(2,1)S(1)}, bf16[96,1024]{1,0:T(8,128)(2,1)S(1)}, f32[96,128]{1,0:T(8,128)S(1)}) custom-call(bf16[80,384]{1,0:T(8,128)(2,1)S(1)} %adapter_down.1.own_ref, bf16[80,384]{1,0:T(8,128)(2,1)S(1)} %add_convert_fusion.1.pair_ref, ...), custom_call_target="tpu_custom_call" | custom-call | flops 805306368 | bytes 2097152 | tf_op jit(solution)/shard_map/adapter_up/pallas_call | solution.py:379
  40.7 0.1 collective-permute-start.9
  40.8 2.8 %collective-permute-start.1 = (bf16[96,1024]{1,0:T(8,128)(2,1)S(1)}, bf16[96,1024]{1,0:T(8,128)(2,1)S(1)}, u32[]{:S(2)}, u32[]{:S(2)}) collective-permute-start(bf16[96,1024]{1,0:T(8,128)(2,1)S(1)} %add_convert_fusion), channel_id=1, source_target_pairs={{0,2},{1,3},{2,0},{3,1},{4,6},{5,7},{6,4},{7,5},{8,10},{9,11},{10,... | collective-permute-start | bytes 589832 | tf_op jit(solution)/shard_map/ppermute | solution.py:416
  43.6 0.2 collective-permute-start.8
  43.8 1.5 %collective-permute-start.10 = (bf16[96,1024]{1,0:T(8,128)(2,1)S(1)}, bf16[96,1024]{1,0:T(8,128)(2,1)S(1)}, u32[]{:S(2)}, u32[]{:S(2)}) collective-permute-start(bf16[96,1024]{1,0:T(8,128)(2,1)S(1)} %add.18), channel_id=1, source_target_pairs={{0,8},{4,12},{8,0},{12,4},{1,9},{5,13},{9,1},{13,5},{2,10},{6,14},... | collective-permute-start | bytes 589832 | tf_op jit(solution)/shard_map/ppermute | solution.py:416
  45.3 0.1 slice_reduce_fusion
  45.4 7.8 %collective-permute-done.1.mid_ref = bf16[96,1024]{1,0:T(8,128)(2,1)S(1)} collective-permute-done((bf16[96,1024]{1,0:T(8,128)(2,1)S(1)}, bf16[96,1024]{1,0:T(8,128)(2,1)S(1)}, u32[]{:S(2)}, u32[]{:S(2)}) %collective-permute-start.1) | collective-permute-done | bytes 196640 | tf_op jit(solution)/shard_map/ppermute | solution.py:416
  53.3 0.1 sum_parts.1
  53.4 0.8 %multiply_convert_fusion = bf16[96,1024]{1,0:T(8,128)(2,1)} fusion(bf16[96,1024]{1,0:T(8,128)(2,1)S(1)} %collective-permute-done.10, f32[96,1024]{1,0:T(8,128)S(1)} %sum_parts.1, bf16[96,1024]{1,0:T(8,128)(2,1)S(1)} %collective-permute-done.5, f32[96]{0:T(128)S(1)} %slice_reduce_fusion), kind=kLoop, calls=%fused_computation | loop fusion | flops 589824 | bytes 983424 | tf_op jit(solution)/shard_map/convert_element_type | solution.py:479
  (13 shorter events, 0.1 us)
Async XLA Ops:
  12.8 12.7 %collective-permute-start.3 = (bf16[96,2176]{1,0:T(8,128)(2,1)S(1)}, bf16[96,2176]{1,0:T(8,128)(2,1)S(1)}, u32[]{:S(2)}, u32[]{:S(2)}) collective-permute-start(bf16[96,2176]{1,0:T(8,128)(2,1)S(1)} %get-tuple-element.21.u_ref.refs_0_), channel_id=1, source_target_pairs={{0,8},{4,12},{8,0},{12,4},{1,9},{5,13},{9,1},{13,5},{2,10},{6,14},... | collective-permute-start | bytes 1253384 | tf_op jit(solution)/shard_map/ppermute | solution.py:416
  15.8 10.1 %collective-permute-start.2 = (bf16[96,2176]{1,0:T(8,128)(2,1)S(1)}, bf16[96,2176]{1,0:T(8,128)(2,1)S(1)}, u32[]{:S(2)}, u32[]{:S(2)}) collective-permute-start(bf16[96,2176]{1,0:T(8,128)(2,1)S(1)} %get-tuple-element.21.u_ref.refs_0_), channel_id=1, source_target_pairs={{0,4},{4,0},{8,12},{12,8},{1,5},{5,1},{9,13},{13,9},{2,6},{6,2},{1... | collective-permute-start | bytes 1253384 | tf_op jit(solution)/shard_map/ppermute | solution.py:416
  18.3 8.9 %copy-start = (bf16[16,2048,64]{1,2,0:T(8,128)(2,1)S(1)}, bf16[16,2048,64]{1,2,0:T(8,128)(2,1)}, u32[]{:S(2)}) copy-start(bf16[16,2048,64]{1,2,0:T(8,128)(2,1)} %param.26) | copy-start | bytes 12582916
  18.3 21.1 %copy-start.1 = (bf16[16,64,1024]{2,1,0:T(8,128)(2,1)S(1)}, bf16[16,64,1024]{2,1,0:T(8,128)(2,1)}, u32[]{:S(2)}) copy-start(bf16[16,64,1024]{2,1,0:T(8,128)(2,1)} %param.27) | copy-start | bytes 6291460
  18.3 7.5 %collective-permute-start = (bf16[96,1024]{1,0:T(8,128)(2,1)S(1)}, bf16[96,1024]{1,0:T(8,128)(2,1)S(1)}, u32[]{:S(2)}, u32[]{:S(2)}) collective-permute-start(bf16[96,1024]{1,0:T(8,128)(2,1)S(1)} %base_first.1), channel_id=1, source_target_pairs={{0,1},{1,0},{2,3},{3,2},{4,5},{5,4},{6,7},{7,6},{8,9},{9,8},{10,11... | collective-permute-start | bytes 589832 | tf_op jit(solution)/shard_map/ppermute | solution.py:416
  25.4 1.8 %collective-permute-start.4 = (bf16[96,2176]{1,0:T(8,128)(2,1)S(1)}, bf16[96,2176]{1,0:T(8,128)(2,1)S(1)}, u32[]{:S(2)}, u32[]{:S(2)}) collective-permute-start(bf16[96,2176]{1,0:T(8,128)(2,1)S(1)} %collective-permute-done.3.refs_2_), channel_id=1, source_target_pairs={{0,4},{4,0},{8,12},{12,8},{1,5},{5,1},{9,13},{13,9},{2,6},{6,2},{1... | collective-permute-start | bytes 1253384 | tf_op jit(solution)/shard_map/ppermute | solution.py:416
  29.6 4.4 %collective-permute-start.6 = (bf16[80,384]{1,0:T(8,128)(2,1)S(1)}, bf16[80,384]{1,0:T(8,128)(2,1)S(1)}, u32[]{:S(2)}, u32[]{:S(2)}) collective-permute-start(bf16[80,384]{1,0:T(8,128)(2,1)S(1)} %adapter_down.1.own_ref), channel_id=1, source_target_pairs={{0,1},{1,0},{2,3},{3,2},{4,5},{5,4},{6,7},{7,6},{8,9},{9,8},{10,11... | collective-permute-start | bytes 184328 | tf_op jit(solution)/shard_map/ppermute | solution.py:416
  31.4 8.0 %collective-permute-start.5 = (bf16[96,1024]{1,0:T(8,128)(2,1)S(1)}, bf16[96,1024]{1,0:T(8,128)(2,1)S(1)}, u32[]{:S(2)}, u32[]{:S(2)}) collective-permute-start(bf16[96,1024]{1,0:T(8,128)(2,1)S(1)} %get-tuple-element.24), channel_id=1, source_target_pairs={{0,1},{1,0},{2,3},{3,2},{4,5},{5,4},{6,7},{7,6},{8,9},{9,8},{10,11... | collective-permute-start | bytes 589832 | tf_op jit(solution)/shard_map/ppermute | solution.py:416
  34.0 5.4 %collective-permute-start.7 = (bf16[80,384]{1,0:T(8,128)(2,1)S(1)}, bf16[80,384]{1,0:T(8,128)(2,1)S(1)}, u32[]{:S(2)}, u32[]{:S(2)}) collective-permute-start(bf16[80,384]{1,0:T(8,128)(2,1)S(1)} %add_convert_fusion.1.pair_ref), channel_id=1, source_target_pairs={{0,2},{1,3},{2,0},{3,1},{4,6},{5,7},{6,4},{7,5},{8,10},{9,11},{10,... | collective-permute-start | bytes 184328 | tf_op jit(solution)/shard_map/ppermute | solution.py:416
  40.7 3.0 %collective-permute-start.9 = (bf16[96,1024]{1,0:T(8,128)(2,1)S(1)}, bf16[96,1024]{1,0:T(8,128)(2,1)S(1)}, u32[]{:S(2)}, u32[]{:S(2)}) collective-permute-start(bf16[96,1024]{1,0:T(8,128)(2,1)S(1)} %get-tuple-element.29), channel_id=1, source_target_pairs={{0,4},{4,0},{8,12},{12,8},{1,5},{5,1},{9,13},{13,9},{2,6},{6,2},{1... | collective-permute-start | bytes 589832 | tf_op jit(solution)/shard_map/ppermute | solution.py:416
  40.8 12.5 %collective-permute-start.1 = (bf16[96,1024]{1,0:T(8,128)(2,1)S(1)}, bf16[96,1024]{1,0:T(8,128)(2,1)S(1)}, u32[]{:S(2)}, u32[]{:S(2)}) collective-permute-start(bf16[96,1024]{1,0:T(8,128)(2,1)S(1)} %add_convert_fusion), channel_id=1, source_target_pairs={{0,2},{1,3},{2,0},{3,1},{4,6},{5,7},{6,4},{7,5},{8,10},{9,11},{10,... | collective-permute-start | bytes 589832 | tf_op jit(solution)/shard_map/ppermute | solution.py:416
  43.6 9.7 %collective-permute-start.8 = (bf16[96,1024]{1,0:T(8,128)(2,1)S(1)}, bf16[96,1024]{1,0:T(8,128)(2,1)S(1)}, u32[]{:S(2)}, u32[]{:S(2)}) collective-permute-start(bf16[96,1024]{1,0:T(8,128)(2,1)S(1)} %get-tuple-element.27), channel_id=1, source_target_pairs={{0,4},{4,0},{8,12},{12,8},{1,5},{5,1},{9,13},{13,9},{2,6},{6,2},{1... | collective-permute-start | bytes 589832 | tf_op jit(solution)/shard_map/ppermute | solution.py:416
  43.8 9.6 %collective-permute-start.10 = (bf16[96,1024]{1,0:T(8,128)(2,1)S(1)}, bf16[96,1024]{1,0:T(8,128)(2,1)S(1)}, u32[]{:S(2)}, u32[]{:S(2)}) collective-permute-start(bf16[96,1024]{1,0:T(8,128)(2,1)S(1)} %add.18), channel_id=1, source_target_pairs={{0,8},{4,12},{8,0},{12,4},{1,9},{5,13},{9,1},{13,5},{2,10},{6,14},... | collective-permute-start | bytes 589832 | tf_op jit(solution)/shard_map/ppermute | solution.py:416
